TPU v7x, 512 devices: a whole 4x4x16 slice. The times are simulated.
512 devices in a mesh: section: 8 (over y, x_lo), lon: 64 (over x_hi, z, core).
Axes of the slice: x: 4 (x_hi: 2, x_lo: 2; x = x_hi * 2 + x_lo), y: 4, z: 16, core: 2. Of those that a mesh axis runs over, the one named last changes fastest.
Arguments:
- inputs: bfloat16 [3, 2, 12, 768, 512], P(None, None, None, 'lon'), may hold values from -6 to 6
- norm_gain: float32 [8, 512], P('section'), may hold values from 0.1 to 1.9
- w_qkv: bfloat16 [8, 512, 1536], P('section'), may hold values from -1.3258252 to 1.3258252
- w_out: bfloat16 [8, 512, 512], P('section'), may hold values from -0.25 to 0.25
- w_head: bfloat16 [512, 1024], P(None, 'section'), may hold values from -0.25 to 0.25
Outputs:
- decoded: bfloat16 [3, 2, 12, 768, 1024], P(None, None, None, 'lon', 'section')
All inputs are finite; a program needn't handle non-finite values.
Results may differ from a plain program's by a relative error of at most 0.019.
Values may be sent and summed in bfloat16 or wider, within the bound.
A program may use at most 64 MiB of HBM per device.

v0:
```python
import jax
import jax.numpy as jnp
from jax import lax
from jax.sharding import PartitionSpec as P

HEADS = 8
WIN_LAT = 6
WIN_LON = 12
SHIFT = 6


EPS = 1e-05


def from_behind(block, axis, distance):
    devices = range(lax.axis_size(axis))
    route = [((i - distance) % len(devices), i) for i in devices]
    return lax.ppermute(block, axis, route)


def passed_along(value, axis, by):
    length = lax.axis_size(axis)
    pairs = [(i, i + by) for i in range(length) if 0 <= i + by < length]
    return lax.ppermute(value, axis, pairs)


def from_root(value, axis, source):
    kept = jnp.where(lax.axis_index(axis) == source, value, 0).astype(value.dtype)
    return lax.psum(kept, axis)


def normalize(field, gain):
    values = field.astype(jnp.float32)
    mean = jnp.mean(values, axis=-1, keepdims=True)
    centred = values - mean
    spread = jnp.mean(centred * centred, axis=-1, keepdims=True)
    return (centred * lax.rsqrt(spread + EPS) * gain).astype(jnp.bfloat16)


def to_windows(field):
    levels, lat, lon, width = field.shape
    blocks = field.reshape(levels, lat // WIN_LAT, WIN_LAT, lon // WIN_LON, WIN_LON, width)
    blocks = blocks.transpose(1, 3, 0, 2, 4, 5)
    return blocks.reshape(-1, levels * WIN_LAT * WIN_LON, width)


def from_windows(blocks, levels, lat, lon):
    width = blocks.shape[-1]
    blocks = blocks.reshape(lat // WIN_LAT, lon // WIN_LON, levels, WIN_LAT, WIN_LON, width)
    return blocks.transpose(2, 0, 3, 1, 4, 5).reshape(levels, lat, lon, width)


def attend(field, gain, w_qkv, w_out):
    levels, lat, lon, width = field.shape
    normed = normalize(field, gain)
    blocks = to_windows(normed)
    count_win, count, _ = blocks.shape
    qkv = jnp.dot(blocks.reshape(-1, width), w_qkv, preferred_element_type=jnp.float32).astype(
        jnp.bfloat16
    )
    qkv = qkv.reshape(count_win, count, 3, HEADS, width // HEADS)
    scores = jnp.einsum(
        "wqhe,wkhe->whqk", qkv[:, :, 0], qkv[:, :, 1], preferred_element_type=jnp.float32
    )
    scores = scores * (width // HEADS) ** (-0.5)
    scores = scores - jnp.max(scores, axis=-1, keepdims=True)
    weights = jnp.exp(scores)
    probs = (weights / jnp.sum(weights, axis=-1, keepdims=True)).astype(jnp.bfloat16)
    mixed = jnp.einsum(
        "whqk,wkhe->wqhe", probs, qkv[:, :, 2], preferred_element_type=jnp.float32
    ).astype(jnp.bfloat16)
    proj = jnp.dot(mixed.reshape(-1, width), w_out, preferred_element_type=jnp.float32)
    back = from_windows(proj.reshape(count_win, count, width), levels, lat, lon)
    return (field.astype(jnp.float32) + back).astype(jnp.bfloat16)


def join_skip(field, partner):
    return (field.astype(jnp.float32) + partner.astype(jnp.float32)).astype(jnp.bfloat16)


def per_device(inputs, norm_gain, w_qkv, w_out, w_head):
    sections = lax.axis_size("section")
    place = lax.axis_index("section")
    micro = inputs.shape[0]
    gain = norm_gain[0]
    weight_qkv = w_qkv[0]
    weight_out = w_out[0]
    first_dec = sections // 2 + sections // 8
    is_decoder = place >= first_dec
    is_shifted = place % 2 == 1
    grid_shape = inputs.shape[1:]
    blank = jnp.zeros(grid_shape, jnp.bfloat16)
    ticks = micro + sections - 1

    def section_block(field):
        ahead = from_behind(field[:, :, :SHIFT], "lon", -1)
        rolled = jnp.concatenate([field[:, :, SHIFT:], ahead], axis=2)
        source = jnp.where(is_shifted, rolled, field)
        result = attend(source, gain, weight_qkv, weight_out)
        behind = from_behind(result[:, :, -SHIFT:], "lon", 1)
        unrolled = jnp.concatenate([behind, result[:, :, :-SHIFT]], axis=2)
        return jnp.where(is_shifted, unrolled, result)

    def entering(step, arriving):
        slot = jnp.clip(step - place, 0, micro - 1)
        fresh = lax.dynamic_index_in_dim(inputs, slot, 0, keepdims=False)
        return jnp.where(place == 0, fresh, arriving)

    def keep(step, saved, result):
        number = step - place
        live = jnp.logical_and(number >= 0, number < micro)
        slot = jnp.clip(number, 0, micro - 1)
        kept = lax.dynamic_update_index_in_dim(saved, result, slot, 0)
        return jnp.where(live, kept, saved)

    saved_init = jnp.zeros((micro,) + grid_shape, jnp.bfloat16)

    def tick(step, state):
        arriving, saved = state
        field = entering(step, arriving)
        pick = jnp.clip(step - (place + first_dec), 0, micro - 1)
        offer = lax.dynamic_index_in_dim(saved, pick, 0, keepdims=False)
        partner = passed_along(offer, "section", first_dec)
        field = jnp.where(is_decoder, join_skip(field, partner), field)
        result = section_block(field)
        saved = keep(step, saved, result)
        arriving = passed_along(result, "section", 1)
        return (arriving, saved)

    _, saved = lax.fori_loop(0, ticks, tick, (blank, saved_init))
    whole = from_root(saved, "section", sections - 1)
    width = whole.shape[-1]
    head = jnp.dot(whole.reshape(-1, width), w_head, preferred_element_type=jnp.float32)
    return head.astype(jnp.bfloat16).reshape(whole.shape[:-1] + (w_head.shape[1],))


def solution(mesh):
    placed = (
        P(None, None, None, "lon", None),
        P("section", None),
        P("section", None, None),
        P("section", None, None),
        P(None, "section"),
    )
    return jax.shard_map(
        per_device,
        mesh=mesh,
        in_specs=placed,
        out_specs=P(None, None, None, "lon", "section"),
        check_vma=False,
    )
```

profile of v0, /device:TPU:4, one launch (start us, length us, event | category | flops | bytes accessed | tf_op | source)
XLA Modules:
  0.0 670.8 jit_solution(10257609978916161789)
XLA Ops:
  8.1 561.6 %while.16 = (s32[]{:T(128)}, bf16[2,12,12,512]{3,0,2,1:T(2,128)(2,1)S(1)}, bf16[3,2,12,12,512]{4,1,3,2,0:T(2,128)(2,1)}, pred[]{:T(512)}, pred[]{:T(512)}, /*ind...) while((s32[]{:T(128)}, ...), condition=%wide.region_5.6_spmd, body=%wide.region_0.5_spmd.sunk | while | flops 695624064 | bytes 38837364 | solution.py:130
  9.3 5.8 collective-permute-start
  15.1 6.2 collective-permute-done
  23.0 10.3 %collective-permute-start.1 = (bf16[2,12,6,512]{3,0,2,1:T(2,128)(2,1)S(1)}, bf16[2,12,6,512]{3,0,2,1:T(2,128)(2,1)S(1)}, u32[]{:S(2)}, u32[]{:S(2)}) collective-permute-start(bf16[2,12,6,512]{3,0,2,1:T(2,128)(2,1)S(1)} %get-tuple-element.358), channel_id=1, source_target_pairs={{1,0},{2,1},{3,2},{4,3},{5,4},{6,5},{7,6},{8,7},{9,8},{10,9},{11,1... | collective-permute-start | bytes 442376 | tf_op jit(solution)/shard_map/while/body/eval_jaxpr/ppermute | solution.py:18
  33.4 2.7 collective-permute-done.1
  50.6 8.3 %collective-permute-done.2 = bf16[2,12,6,512]{3,0,2,1:T(2,128)(2,1)S(1)} collective-permute-done((bf16[2,12,6,512]{3,0,2,1:T(2,128)(2,1)S(1)}, bf16[2,12,6,512]{3,0,2,1:T(2,128)(2,1)S(1)}, u32[]{:S(2)}, u32[]{:S(2)}) %collective-permute-start.2) | collective-permute-done | bytes 147488 | tf_op jit(solution)/shard_map/while/body/eval_jaxpr/ppermute | solution.py:18
  61.1 2.9 collective-permute-start.3
  64.0 4.2 collective-permute-done.3
  69.4 8.9 %collective-permute-start = (bf16[2,12,12,512]{3,0,2,1:T(2,128)(2,1)S(1)}, bf16[2,12,12,512]{3,0,2,1:T(2,128)(2,1)S(1)}, u32[]{:S(2)}, u32[]{:S(2)}) collective-permute-start(bf16[2,12,12,512]{3,0,2,1:T(2,128)(2,1)S(1)} %dynamic-slice_bitcast_fusion.2), channel_id=1, source_target_pairs={{0,320},{64,384},{128,448},{1,321},{65,385},{129,449},{2,322},{66,... | collective-permute-start | bytes 884744 | tf_op jit(solution)/shard_map/while/body/eval_jaxpr/ppermute | solution.py:24
  78.4 4.2 collective-permute-done
  84.3 4.2 collective-permute-start.1
  105.7 8.3 %collective-permute-done.2 = bf16[2,12,6,512]{3,0,2,1:T(2,128)(2,1)S(1)} collective-permute-done((bf16[2,12,6,512]{3,0,2,1:T(2,128)(2,1)S(1)}, bf16[2,12,6,512]{3,0,2,1:T(2,128)(2,1)S(1)}, u32[]{:S(2)}, u32[]{:S(2)}) %collective-permute-start.2) | collective-permute-done | bytes 147488 | tf_op jit(solution)/shard_map/while/body/eval_jaxpr/ppermute | solution.py:18
  116.3 3.5 collective-permute-start.3
  119.7 4.2 collective-permute-done.3
  125.1 8.3 %collective-permute-start = (bf16[2,12,12,512]{3,0,2,1:T(2,128)(2,1)S(1)}, bf16[2,12,12,512]{3,0,2,1:T(2,128)(2,1)S(1)}, u32[]{:S(2)}, u32[]{:S(2)}) collective-permute-start(bf16[2,12,12,512]{3,0,2,1:T(2,128)(2,1)S(1)} %dynamic-slice_bitcast_fusion.2), channel_id=1, source_target_pairs={{0,320},{64,384},{128,448},{1,321},{65,385},{129,449},{2,322},{66,... | collective-permute-start | bytes 884744 | tf_op jit(solution)/shard_map/while/body/eval_jaxpr/ppermute | solution.py:24
  133.5 4.2 collective-permute-done
  139.4 4.2 collective-permute-start.1
  160.8 8.3 %collective-permute-done.2 = bf16[2,12,6,512]{3,0,2,1:T(2,128)(2,1)S(1)} collective-permute-done((bf16[2,12,6,512]{3,0,2,1:T(2,128)(2,1)S(1)}, bf16[2,12,6,512]{3,0,2,1:T(2,128)(2,1)S(1)}, u32[]{:S(2)}, u32[]{:S(2)}) %collective-permute-start.2) | collective-permute-done | bytes 147488 | tf_op jit(solution)/shard_map/while/body/eval_jaxpr/ppermute | solution.py:18
  171.4 4.1 collective-permute-start.3
  175.5 4.2 collective-permute-done.3
  180.8 7.7 %collective-permute-start = (bf16[2,12,12,512]{3,0,2,1:T(2,128)(2,1)S(1)}, bf16[2,12,12,512]{3,0,2,1:T(2,128)(2,1)S(1)}, u32[]{:S(2)}, u32[]{:S(2)}) collective-permute-start(bf16[2,12,12,512]{3,0,2,1:T(2,128)(2,1)S(1)} %dynamic-slice_bitcast_fusion.2), channel_id=1, source_target_pairs={{0,320},{64,384},{128,448},{1,321},{65,385},{129,449},{2,322},{66,... | collective-permute-start | bytes 884744 | tf_op jit(solution)/shard_map/while/body/eval_jaxpr/ppermute | solution.py:24
  188.6 4.2 collective-permute-done
  194.5 4.2 collective-permute-start.1
  215.9 8.3 %collective-permute-done.2 = bf16[2,12,6,512]{3,0,2,1:T(2,128)(2,1)S(1)} collective-permute-done((bf16[2,12,6,512]{3,0,2,1:T(2,128)(2,1)S(1)}, bf16[2,12,6,512]{3,0,2,1:T(2,128)(2,1)S(1)}, u32[]{:S(2)}, u32[]{:S(2)}) %collective-permute-start.2) | collective-permute-done | bytes 147488 | tf_op jit(solution)/shard_map/while/body/eval_jaxpr/ppermute | solution.py:18
  226.5 4.7 collective-permute-start.3
  231.2 4.2 collective-permute-done.3
  236.6 7.1 %collective-permute-start = (bf16[2,12,12,512]{3,0,2,1:T(2,128)(2,1)S(1)}, bf16[2,12,12,512]{3,0,2,1:T(2,128)(2,1)S(1)}, u32[]{:S(2)}, u32[]{:S(2)}) collective-permute-start(bf16[2,12,12,512]{3,0,2,1:T(2,128)(2,1)S(1)} %dynamic-slice_bitcast_fusion.2), channel_id=1, source_target_pairs={{0,320},{64,384},{128,448},{1,321},{65,385},{129,449},{2,322},{66,... | collective-permute-start | bytes 884744 | tf_op jit(solution)/shard_map/while/body/eval_jaxpr/ppermute | solution.py:24
  243.7 4.2 collective-permute-done
  249.6 4.9 collective-permute-start.1
  271.7 8.3 %collective-permute-done.2 = bf16[2,12,6,512]{3,0,2,1:T(2,128)(2,1)S(1)} collective-permute-done((bf16[2,12,6,512]{3,0,2,1:T(2,128)(2,1)S(1)}, bf16[2,12,6,512]{3,0,2,1:T(2,128)(2,1)S(1)}, u32[]{:S(2)}, u32[]{:S(2)}) %collective-permute-start.2) | collective-permute-done | bytes 147488 | tf_op jit(solution)/shard_map/while/body/eval_jaxpr/ppermute | solution.py:18
  282.3 4.6 collective-permute-start.3
  286.9 4.2 collective-permute-done.3
  292.3 7.2 %collective-permute-start = (bf16[2,12,12,512]{3,0,2,1:T(2,128)(2,1)S(1)}, bf16[2,12,12,512]{3,0,2,1:T(2,128)(2,1)S(1)}, u32[]{:S(2)}, u32[]{:S(2)}) collective-permute-start(bf16[2,12,12,512]{3,0,2,1:T(2,128)(2,1)S(1)} %dynamic-slice_bitcast_fusion.2), channel_id=1, source_target_pairs={{0,320},{64,384},{128,448},{1,321},{65,385},{129,449},{2,322},{66,... | collective-permute-start | bytes 884744 | tf_op jit(solution)/shard_map/while/body/eval_jaxpr/ppermute | solution.py:24
  299.5 4.2 collective-permute-done
  305.4 4.8 collective-permute-start.1
  327.4 8.3 %collective-permute-done.2 = bf16[2,12,6,512]{3,0,2,1:T(2,128)(2,1)S(1)} collective-permute-done((bf16[2,12,6,512]{3,0,2,1:T(2,128)(2,1)S(1)}, bf16[2,12,6,512]{3,0,2,1:T(2,128)(2,1)S(1)}, u32[]{:S(2)}, u32[]{:S(2)}) %collective-permute-start.2) | collective-permute-done | bytes 147488 | tf_op jit(solution)/shard_map/while/body/eval_jaxpr/ppermute | solution.py:18
  338.0 4.6 collective-permute-start.3
  342.6 4.2 collective-permute-done.3
  348.0 7.2 %collective-permute-start = (bf16[2,12,12,512]{3,0,2,1:T(2,128)(2,1)S(1)}, bf16[2,12,12,512]{3,0,2,1:T(2,128)(2,1)S(1)}, u32[]{:S(2)}, u32[]{:S(2)}) collective-permute-start(bf16[2,12,12,512]{3,0,2,1:T(2,128)(2,1)S(1)} %dynamic-slice_bitcast_fusion.2), channel_id=1, source_target_pairs={{0,320},{64,384},{128,448},{1,321},{65,385},{129,449},{2,322},{66,... | collective-permute-start | bytes 884744 | tf_op jit(solution)/shard_map/while/body/eval_jaxpr/ppermute | solution.py:24
  355.2 4.2 collective-permute-done
  361.2 4.8 collective-permute-start.1
  383.2 8.3 %collective-permute-done.2 = bf16[2,12,6,512]{3,0,2,1:T(2,128)(2,1)S(1)} collective-permute-done((bf16[2,12,6,512]{3,0,2,1:T(2,128)(2,1)S(1)}, bf16[2,12,6,512]{3,0,2,1:T(2,128)(2,1)S(1)}, u32[]{:S(2)}, u32[]{:S(2)}) %collective-permute-start.2) | collective-permute-done | bytes 147488 | tf_op jit(solution)/shard_map/while/body/eval_jaxpr/ppermute | solution.py:18
  393.7 4.6 collective-permute-start.3
  398.3 4.2 collective-permute-done.3
  403.7 7.2 %collective-permute-start = (bf16[2,12,12,512]{3,0,2,1:T(2,128)(2,1)S(1)}, bf16[2,12,12,512]{3,0,2,1:T(2,128)(2,1)S(1)}, u32[]{:S(2)}, u32[]{:S(2)}) collective-permute-start(bf16[2,12,12,512]{3,0,2,1:T(2,128)(2,1)S(1)} %dynamic-slice_bitcast_fusion.2), channel_id=1, source_target_pairs={{0,320},{64,384},{128,448},{1,321},{65,385},{129,449},{2,322},{66,... | collective-permute-start | bytes 884744 | tf_op jit(solution)/shard_map/while/body/eval_jaxpr/ppermute | solution.py:24
  411.0 4.2 collective-permute-done
  416.9 4.8 collective-permute-start.1
  438.9 8.3 %collective-permute-done.2 = bf16[2,12,6,512]{3,0,2,1:T(2,128)(2,1)S(1)} collective-permute-done((bf16[2,12,6,512]{3,0,2,1:T(2,128)(2,1)S(1)}, bf16[2,12,6,512]{3,0,2,1:T(2,128)(2,1)S(1)}, u32[]{:S(2)}, u32[]{:S(2)}) %collective-permute-start.2) | collective-permute-done | bytes 147488 | tf_op jit(solution)/shard_map/while/body/eval_jaxpr/ppermute | solution.py:18
  449.5 4.6 collective-permute-start.3
  454.0 4.2 collective-permute-done.3
  459.4 7.2 %collective-permute-start = (bf16[2,12,12,512]{3,0,2,1:T(2,128)(2,1)S(1)}, bf16[2,12,12,512]{3,0,2,1:T(2,128)(2,1)S(1)}, u32[]{:S(2)}, u32[]{:S(2)}) collective-permute-start(bf16[2,12,12,512]{3,0,2,1:T(2,128)(2,1)S(1)} %dynamic-slice_bitcast_fusion.2), channel_id=1, source_target_pairs={{0,320},{64,384},{128,448},{1,321},{65,385},{129,449},{2,322},{66,... | collective-permute-start | bytes 884744 | tf_op jit(solution)/shard_map/while/body/eval_jaxpr/ppermute | solution.py:24
  466.7 4.2 collective-permute-done
  472.6 4.8 collective-permute-start.1
  477.4 2.7 collective-permute-done.1
  494.6 8.3 %collective-permute-done.2 = bf16[2,12,6,512]{3,0,2,1:T(2,128)(2,1)S(1)} collective-permute-done((bf16[2,12,6,512]{3,0,2,1:T(2,128)(2,1)S(1)}, bf16[2,12,6,512]{3,0,2,1:T(2,128)(2,1)S(1)}, u32[]{:S(2)}, u32[]{:S(2)}) %collective-permute-start.2) | collective-permute-done | bytes 147488 | tf_op jit(solution)/shard_map/while/body/eval_jaxpr/ppermute | solution.py:18
  505.2 4.6 collective-permute-start.3
  509.8 4.2 collective-permute-done.3
  515.2 7.2 %collective-permute-start = (bf16[2,12,12,512]{3,0,2,1:T(2,128)(2,1)S(1)}, bf16[2,12,12,512]{3,0,2,1:T(2,128)(2,1)S(1)}, u32[]{:S(2)}, u32[]{:S(2)}) collective-permute-start(bf16[2,12,12,512]{3,0,2,1:T(2,128)(2,1)S(1)} %dynamic-slice_bitcast_fusion.2), channel_id=1, source_target_pairs={{0,320},{64,384},{128,448},{1,321},{65,385},{129,449},{2,322},{66,... | collective-permute-start | bytes 884744 | tf_op jit(solution)/shard_map/while/body/eval_jaxpr/ppermute | solution.py:24
  522.4 4.2 collective-permute-done
  528.3 4.8 collective-permute-start.1
  550.3 8.3 %collective-permute-done.2 = bf16[2,12,6,512]{3,0,2,1:T(2,128)(2,1)S(1)} collective-permute-done((bf16[2,12,6,512]{3,0,2,1:T(2,128)(2,1)S(1)}, bf16[2,12,6,512]{3,0,2,1:T(2,128)(2,1)S(1)}, u32[]{:S(2)}, u32[]{:S(2)}) %collective-permute-start.2) | collective-permute-done | bytes 147488 | tf_op jit(solution)/shard_map/while/body/eval_jaxpr/ppermute | solution.py:18
  560.9 4.6 collective-permute-start.3
  565.5 4.2 collective-permute-done.3
  571.8 89.6 %all-reduce.2.cloned.1.call-done = bf16[864,512]{1,0:T(8,128)(2,1)} async-done(((bf16[864,512]{1,0:T(8,128)(2,1)}), bf16[864,512]{1,0:T(8,128)(2,1)}) %all-reduce.2.cloned.1.call-update) | async-done | bytes 884752 | tf_op jit(solution)/shard_map/psum | solution.py:29
  (350 shorter events, 222.5 us)
Async XLA Ops:
  6.5 654.9 %copy-start = (bf16[512,128]{1,0:T(8,128)(2,1)S(1)}, bf16[512,128]{1,0:T(8,128)(2,1)}, u32[]{:S(2)}) copy-start(bf16[512,128]{1,0:T(8,128)(2,1)} %param.11) | copy-start | bytes 393220
  6.5 654.9 %all-reduce.2.cloned.1.call-start = ((), (), s32[]{:S(2)}) async-start(), calls=%async_computation | async-start | bytes 1769472 | tf_op jit(solution)/shard_map/psum | solution.py:29
  8.1 29.1 %copy-start.2 = (f32[1,512]{1,0:T(1,128)S(1)}, f32[1,512]{1,0:T(1,128)}, u32[]{:S(2)}) copy-start(f32[1,512]{1,0:T(1,128)} %get-tuple-element.412) | copy-start | bytes 6148 | tf_op jit(solution)/shard_map/while
  9.3 12.0 %collective-permute-start = (bf16[2,12,12,512]{3,0,2,1:T(2,128)(2,1)S(1)}, bf16[2,12,12,512]{3,0,2,1:T(2,128)(2,1)S(1)}, u32[]{:S(2)}, u32[]{:S(2)}) collective-permute-start(bf16[2,12,12,512]{3,0,2,1:T(2,128)(2,1)S(1)} %dynamic-slice_bitcast_fusion.2), channel_id=1, source_target_pairs={{0,320},{64,384},{128,448},{1,321},{65,385},{129,449},{2,322},{66,... | collective-permute-start | bytes 884744 | tf_op jit(solution)/shard_map/while/body/eval_jaxpr/ppermute | solution.py:24
  22.8 15.1 %copy-start.3 = (bf16[512,1536]{1,0:T(8,128)(2,1)S(1)}, bf16[512,1536]{1,0:T(8,128)(2,1)}, u32[]{:S(2)}) copy-start(bf16[512,1536]{1,0:T(8,128)(2,1)} %get-tuple-element.413) | copy-start | bytes 4718596 | tf_op jit(solution)/shard_map/while
  23.0 13.0 %collective-permute-start.1 = (bf16[2,12,6,512]{3,0,2,1:T(2,128)(2,1)S(1)}, bf16[2,12,6,512]{3,0,2,1:T(2,128)(2,1)S(1)}, u32[]{:S(2)}, u32[]{:S(2)}) collective-permute-start(bf16[2,12,6,512]{3,0,2,1:T(2,128)(2,1)S(1)} %get-tuple-element.358), channel_id=1, source_target_pairs={{1,0},{2,1},{3,2},{4,3},{5,4},{6,5},{7,6},{8,7},{9,8},{10,9},{11,1... | collective-permute-start | bytes 442376 | tf_op jit(solution)/shard_map/while/body/eval_jaxpr/ppermute | solution.py:18
  46.2 1.0 copy-start.1
  48.6 10.2 %collective-permute-start.2 = (bf16[2,12,6,512]{3,0,2,1:T(2,128)(2,1)S(1)}, bf16[2,12,6,512]{3,0,2,1:T(2,128)(2,1)S(1)}, u32[]{:S(2)}, u32[]{:S(2)}) collective-permute-start(bf16[2,12,6,512]{3,0,2,1:T(2,128)(2,1)S(1)} %get-tuple-element.368), channel_id=1, source_target_pairs={{63,0},{0,1},{1,2},{2,3},{3,4},{4,5},{5,6},{6,7},{7,8},{8,9},{9,10... | collective-permute-start | bytes 442376 | tf_op jit(solution)/shard_map/while/body/eval_jaxpr/ppermute | solution.py:18
  61.1 7.1 %collective-permute-start.3 = (bf16[2,12,12,512]{3,0,2,1:T(2,128)(2,1)S(1)}, bf16[2,12,12,512]{3,0,2,1:T(2,128)(2,1)S(1)}, u32[]{:S(2)}, u32[]{:S(2)}) collective-permute-start(bf16[2,12,12,512]{3,0,2,1:T(2,128)(2,1)S(1)} %get-tuple-element.369), channel_id=1, source_target_pairs={{0,64},{64,128},{128,192},{192,256},{256,320},{320,384},{384,448},... | collective-permute-start | bytes 884744 | tf_op jit(solution)/shard_map/while/body/eval_jaxpr/ppermute | solution.py:24
  68.2 24.2 %copy-start.2 = (f32[1,512]{1,0:T(1,128)S(1)}, f32[1,512]{1,0:T(1,128)}, u32[]{:S(2)}) copy-start(f32[1,512]{1,0:T(1,128)} %get-tuple-element.412) | copy-start | bytes 6148 | tf_op jit(solution)/shard_map/while
  69.4 13.1 %collective-permute-start = (bf16[2,12,12,512]{3,0,2,1:T(2,128)(2,1)S(1)}, bf16[2,12,12,512]{3,0,2,1:T(2,128)(2,1)S(1)}, u32[]{:S(2)}, u32[]{:S(2)}) collective-permute-start(bf16[2,12,12,512]{3,0,2,1:T(2,128)(2,1)S(1)} %dynamic-slice_bitcast_fusion.2), channel_id=1, source_target_pairs={{0,320},{64,384},{128,448},{1,321},{65,385},{129,449},{2,322},{66,... | collective-permute-start | bytes 884744 | tf_op jit(solution)/shard_map/while/body/eval_jaxpr/ppermute | solution.py:24
  84.1 8.9 %copy-start.3 = (bf16[512,1536]{1,0:T(8,128)(2,1)S(1)}, bf16[512,1536]{1,0:T(8,128)(2,1)}, u32[]{:S(2)}) copy-start(bf16[512,1536]{1,0:T(8,128)(2,1)} %get-tuple-element.413) | copy-start | bytes 4718596 | tf_op jit(solution)/shard_map/while
  84.3 6.9 %collective-permute-start.1 = (bf16[2,12,6,512]{3,0,2,1:T(2,128)(2,1)S(1)}, bf16[2,12,6,512]{3,0,2,1:T(2,128)(2,1)S(1)}, u32[]{:S(2)}, u32[]{:S(2)}) collective-permute-start(bf16[2,12,6,512]{3,0,2,1:T(2,128)(2,1)S(1)} %get-tuple-element.358), channel_id=1, source_target_pairs={{1,0},{2,1},{3,2},{4,3},{5,4},{6,5},{7,6},{8,7},{9,8},{10,9},{11,1... | collective-permute-start | bytes 442376 | tf_op jit(solution)/shard_map/while/body/eval_jaxpr/ppermute | solution.py:18
  101.3 1.0 copy-start.1
  103.7 10.2 %collective-permute-start.2 = (bf16[2,12,6,512]{3,0,2,1:T(2,128)(2,1)S(1)}, bf16[2,12,6,512]{3,0,2,1:T(2,128)(2,1)S(1)}, u32[]{:S(2)}, u32[]{:S(2)}) collective-permute-start(bf16[2,12,6,512]{3,0,2,1:T(2,128)(2,1)S(1)} %get-tuple-element.368), channel_id=1, source_target_pairs={{63,0},{0,1},{1,2},{2,3},{3,4},{4,5},{5,6},{6,7},{7,8},{8,9},{9,10... | collective-permute-start | bytes 442376 | tf_op jit(solution)/shard_map/while/body/eval_jaxpr/ppermute | solution.py:18
  116.3 7.7 %collective-permute-start.3 = (bf16[2,12,12,512]{3,0,2,1:T(2,128)(2,1)S(1)}, bf16[2,12,12,512]{3,0,2,1:T(2,128)(2,1)S(1)}, u32[]{:S(2)}, u32[]{:S(2)}) collective-permute-start(bf16[2,12,12,512]{3,0,2,1:T(2,128)(2,1)S(1)} %get-tuple-element.369), channel_id=1, source_target_pairs={{0,64},{64,128},{128,192},{192,256},{256,320},{320,384},{384,448},... | collective-permute-start | bytes 884744 | tf_op jit(solution)/shard_map/while/body/eval_jaxpr/ppermute | solution.py:24
  123.9 23.6 %copy-start.2 = (f32[1,512]{1,0:T(1,128)S(1)}, f32[1,512]{1,0:T(1,128)}, u32[]{:S(2)}) copy-start(f32[1,512]{1,0:T(1,128)} %get-tuple-element.412) | copy-start | bytes 6148 | tf_op jit(solution)/shard_map/while
  125.1 12.5 %collective-permute-start = (bf16[2,12,12,512]{3,0,2,1:T(2,128)(2,1)S(1)}, bf16[2,12,12,512]{3,0,2,1:T(2,128)(2,1)S(1)}, u32[]{:S(2)}, u32[]{:S(2)}) collective-permute-start(bf16[2,12,12,512]{3,0,2,1:T(2,128)(2,1)S(1)} %dynamic-slice_bitcast_fusion.2), channel_id=1, source_target_pairs={{0,320},{64,384},{128,448},{1,321},{65,385},{129,449},{2,322},{66,... | collective-permute-start | bytes 884744 | tf_op jit(solution)/shard_map/while/body/eval_jaxpr/ppermute | solution.py:24
  139.2 8.9 %copy-start.3 = (bf16[512,1536]{1,0:T(8,128)(2,1)S(1)}, bf16[512,1536]{1,0:T(8,128)(2,1)}, u32[]{:S(2)}) copy-start(bf16[512,1536]{1,0:T(8,128)(2,1)} %get-tuple-element.413) | copy-start | bytes 4718596 | tf_op jit(solution)/shard_map/while
  139.4 6.9 %collective-permute-start.1 = (bf16[2,12,6,512]{3,0,2,1:T(2,128)(2,1)S(1)}, bf16[2,12,6,512]{3,0,2,1:T(2,128)(2,1)S(1)}, u32[]{:S(2)}, u32[]{:S(2)}) collective-permute-start(bf16[2,12,6,512]{3,0,2,1:T(2,128)(2,1)S(1)} %get-tuple-element.358), channel_id=1, source_target_pairs={{1,0},{2,1},{3,2},{4,3},{5,4},{6,5},{7,6},{8,7},{9,8},{10,9},{11,1... | collective-permute-start | bytes 442376 | tf_op jit(solution)/shard_map/while/body/eval_jaxpr/ppermute | solution.py:18
  158.9 10.2 %collective-permute-start.2 = (bf16[2,12,6,512]{3,0,2,1:T(2,128)(2,1)S(1)}, bf16[2,12,6,512]{3,0,2,1:T(2,128)(2,1)S(1)}, u32[]{:S(2)}, u32[]{:S(2)}) collective-permute-start(bf16[2,12,6,512]{3,0,2,1:T(2,128)(2,1)S(1)} %get-tuple-element.368), channel_id=1, source_target_pairs={{63,0},{0,1},{1,2},{2,3},{3,4},{4,5},{5,6},{6,7},{7,8},{8,9},{9,10... | collective-permute-start | bytes 442376 | tf_op jit(solution)/shard_map/while/body/eval_jaxpr/ppermute | solution.py:18
  171.4 8.3 %collective-permute-start.3 = (bf16[2,12,12,512]{3,0,2,1:T(2,128)(2,1)S(1)}, bf16[2,12,12,512]{3,0,2,1:T(2,128)(2,1)S(1)}, u32[]{:S(2)}, u32[]{:S(2)}) collective-permute-start(bf16[2,12,12,512]{3,0,2,1:T(2,128)(2,1)S(1)} %get-tuple-element.369), channel_id=1, source_target_pairs={{0,64},{64,128},{128,192},{192,256},{256,320},{320,384},{384,448},... | collective-permute-start | bytes 884744 | tf_op jit(solution)/shard_map/while/body/eval_jaxpr/ppermute | solution.py:24
  179.7 23.0 %copy-start.2 = (f32[1,512]{1,0:T(1,128)S(1)}, f32[1,512]{1,0:T(1,128)}, u32[]{:S(2)}) copy-start(f32[1,512]{1,0:T(1,128)} %get-tuple-element.412) | copy-start | bytes 6148 | tf_op jit(solution)/shard_map/while
  180.8 11.9 %collective-permute-start = (bf16[2,12,12,512]{3,0,2,1:T(2,128)(2,1)S(1)}, bf16[2,12,12,512]{3,0,2,1:T(2,128)(2,1)S(1)}, u32[]{:S(2)}, u32[]{:S(2)}) collective-permute-start(bf16[2,12,12,512]{3,0,2,1:T(2,128)(2,1)S(1)} %dynamic-slice_bitcast_fusion.2), channel_id=1, source_target_pairs={{0,320},{64,384},{128,448},{1,321},{65,385},{129,449},{2,322},{66,... | collective-permute-start | bytes 884744 | tf_op jit(solution)/shard_map/while/body/eval_jaxpr/ppermute | solution.py:24
  194.3 8.9 %copy-start.3 = (bf16[512,1536]{1,0:T(8,128)(2,1)S(1)}, bf16[512,1536]{1,0:T(8,128)(2,1)}, u32[]{:S(2)}) copy-start(bf16[512,1536]{1,0:T(8,128)(2,1)} %get-tuple-element.413) | copy-start | bytes 4718596 | tf_op jit(solution)/shard_map/while
  194.5 6.9 %collective-permute-start.1 = (bf16[2,12,6,512]{3,0,2,1:T(2,128)(2,1)S(1)}, bf16[2,12,6,512]{3,0,2,1:T(2,128)(2,1)S(1)}, u32[]{:S(2)}, u32[]{:S(2)}) collective-permute-start(bf16[2,12,6,512]{3,0,2,1:T(2,128)(2,1)S(1)} %get-tuple-element.358), channel_id=1, source_target_pairs={{1,0},{2,1},{3,2},{4,3},{5,4},{6,5},{7,6},{8,7},{9,8},{10,9},{11,1... | collective-permute-start | bytes 442376 | tf_op jit(solution)/shard_map/while/body/eval_jaxpr/ppermute | solution.py:18
  214.0 10.2 %collective-permute-start.2 = (bf16[2,12,6,512]{3,0,2,1:T(2,128)(2,1)S(1)}, bf16[2,12,6,512]{3,0,2,1:T(2,128)(2,1)S(1)}, u32[]{:S(2)}, u32[]{:S(2)}) collective-permute-start(bf16[2,12,6,512]{3,0,2,1:T(2,128)(2,1)S(1)} %get-tuple-element.368), channel_id=1, source_target_pairs={{63,0},{0,1},{1,2},{2,3},{3,4},{4,5},{5,6},{6,7},{7,8},{8,9},{9,10... | collective-permute-start | bytes 442376 | tf_op jit(solution)/shard_map/while/body/eval_jaxpr/ppermute | solution.py:18
  226.5 8.9 %collective-permute-start.3 = (bf16[2,12,12,512]{3,0,2,1:T(2,128)(2,1)S(1)}, bf16[2,12,12,512]{3,0,2,1:T(2,128)(2,1)S(1)}, u32[]{:S(2)}, u32[]{:S(2)}) collective-permute-start(bf16[2,12,12,512]{3,0,2,1:T(2,128)(2,1)S(1)} %get-tuple-element.369), channel_id=1, source_target_pairs={{0,64},{64,128},{128,192},{192,256},{256,320},{320,384},{384,448},... | collective-permute-start | bytes 884744 | tf_op jit(solution)/shard_map/while/body/eval_jaxpr/ppermute | solution.py:24
  235.4 23.1 %copy-start.2 = (f32[1,512]{1,0:T(1,128)S(1)}, f32[1,512]{1,0:T(1,128)}, u32[]{:S(2)}) copy-start(f32[1,512]{1,0:T(1,128)} %get-tuple-element.412) | copy-start | bytes 6148 | tf_op jit(solution)/shard_map/while
  236.6 11.3 %collective-permute-start = (bf16[2,12,12,512]{3,0,2,1:T(2,128)(2,1)S(1)}, bf16[2,12,12,512]{3,0,2,1:T(2,128)(2,1)S(1)}, u32[]{:S(2)}, u32[]{:S(2)}) collective-permute-start(bf16[2,12,12,512]{3,0,2,1:T(2,128)(2,1)S(1)} %dynamic-slice_bitcast_fusion.2), channel_id=1, source_target_pairs={{0,320},{64,384},{128,448},{1,321},{65,385},{129,449},{2,322},{66,... | collective-permute-start | bytes 884744 | tf_op jit(solution)/shard_map/while/body/eval_jaxpr/ppermute | solution.py:24
  249.4 9.6 %copy-start.3 = (bf16[512,1536]{1,0:T(8,128)(2,1)S(1)}, bf16[512,1536]{1,0:T(8,128)(2,1)}, u32[]{:S(2)}) copy-start(bf16[512,1536]{1,0:T(8,128)(2,1)} %get-tuple-element.413) | copy-start | bytes 4718596 | tf_op jit(solution)/shard_map/while
  249.6 7.6 %collective-permute-start.1 = (bf16[2,12,6,512]{3,0,2,1:T(2,128)(2,1)S(1)}, bf16[2,12,6,512]{3,0,2,1:T(2,128)(2,1)S(1)}, u32[]{:S(2)}, u32[]{:S(2)}) collective-permute-start(bf16[2,12,6,512]{3,0,2,1:T(2,128)(2,1)S(1)} %get-tuple-element.358), channel_id=1, source_target_pairs={{1,0},{2,1},{3,2},{4,3},{5,4},{6,5},{7,6},{8,7},{9,8},{10,9},{11,1... | collective-permute-start | bytes 442376 | tf_op jit(solution)/shard_map/while/body/eval_jaxpr/ppermute | solution.py:18
  269.8 10.2 %collective-permute-start.2 = (bf16[2,12,6,512]{3,0,2,1:T(2,128)(2,1)S(1)}, bf16[2,12,6,512]{3,0,2,1:T(2,128)(2,1)S(1)}, u32[]{:S(2)}, u32[]{:S(2)}) collective-permute-start(bf16[2,12,6,512]{3,0,2,1:T(2,128)(2,1)S(1)} %get-tuple-element.368), channel_id=1, source_target_pairs={{63,0},{0,1},{1,2},{2,3},{3,4},{4,5},{5,6},{6,7},{7,8},{8,9},{9,10... | collective-permute-start | bytes 442376 | tf_op jit(solution)/shard_map/while/body/eval_jaxpr/ppermute | solution.py:18
  282.3 8.8 %collective-permute-start.3 = (bf16[2,12,12,512]{3,0,2,1:T(2,128)(2,1)S(1)}, bf16[2,12,12,512]{3,0,2,1:T(2,128)(2,1)S(1)}, u32[]{:S(2)}, u32[]{:S(2)}) collective-permute-start(bf16[2,12,12,512]{3,0,2,1:T(2,128)(2,1)S(1)} %get-tuple-element.369), channel_id=1, source_target_pairs={{0,64},{64,128},{128,192},{192,256},{256,320},{320,384},{384,448},... | collective-permute-start | bytes 884744 | tf_op jit(solution)/shard_map/while/body/eval_jaxpr/ppermute | solution.py:24
  291.1 23.1 %copy-start.2 = (f32[1,512]{1,0:T(1,128)S(1)}, f32[1,512]{1,0:T(1,128)}, u32[]{:S(2)}) copy-start(f32[1,512]{1,0:T(1,128)} %get-tuple-element.412) | copy-start | bytes 6148 | tf_op jit(solution)/shard_map/while
  292.3 11.4 %collective-permute-start = (bf16[2,12,12,512]{3,0,2,1:T(2,128)(2,1)S(1)}, bf16[2,12,12,512]{3,0,2,1:T(2,128)(2,1)S(1)}, u32[]{:S(2)}, u32[]{:S(2)}) collective-permute-start(bf16[2,12,12,512]{3,0,2,1:T(2,128)(2,1)S(1)} %dynamic-slice_bitcast_fusion.2), channel_id=1, source_target_pairs={{0,320},{64,384},{128,448},{1,321},{65,385},{129,449},{2,322},{66,... | collective-permute-start | bytes 884744 | tf_op jit(solution)/shard_map/while/body/eval_jaxpr/ppermute | solution.py:24
  305.2 9.5 %copy-start.3 = (bf16[512,1536]{1,0:T(8,128)(2,1)S(1)}, bf16[512,1536]{1,0:T(8,128)(2,1)}, u32[]{:S(2)}) copy-start(bf16[512,1536]{1,0:T(8,128)(2,1)} %get-tuple-element.413) | copy-start | bytes 4718596 | tf_op jit(solution)/shard_map/while
  305.4 7.5 %collective-permute-start.1 = (bf16[2,12,6,512]{3,0,2,1:T(2,128)(2,1)S(1)}, bf16[2,12,6,512]{3,0,2,1:T(2,128)(2,1)S(1)}, u32[]{:S(2)}, u32[]{:S(2)}) collective-permute-start(bf16[2,12,6,512]{3,0,2,1:T(2,128)(2,1)S(1)} %get-tuple-element.358), channel_id=1, source_target_pairs={{1,0},{2,1},{3,2},{4,3},{5,4},{6,5},{7,6},{8,7},{9,8},{10,9},{11,1... | collective-permute-start | bytes 442376 | tf_op jit(solution)/shard_map/while/body/eval_jaxpr/ppermute | solution.py:18
  325.5 10.2 %collective-permute-start.2 = (bf16[2,12,6,512]{3,0,2,1:T(2,128)(2,1)S(1)}, bf16[2,12,6,512]{3,0,2,1:T(2,128)(2,1)S(1)}, u32[]{:S(2)}, u32[]{:S(2)}) collective-permute-start(bf16[2,12,6,512]{3,0,2,1:T(2,128)(2,1)S(1)} %get-tuple-element.368), channel_id=1, source_target_pairs={{63,0},{0,1},{1,2},{2,3},{3,4},{4,5},{5,6},{6,7},{7,8},{8,9},{9,10... | collective-permute-start | bytes 442376 | tf_op jit(solution)/shard_map/while/body/eval_jaxpr/ppermute | solution.py:18
  338.0 8.8 %collective-permute-start.3 = (bf16[2,12,12,512]{3,0,2,1:T(2,128)(2,1)S(1)}, bf16[2,12,12,512]{3,0,2,1:T(2,128)(2,1)S(1)}, u32[]{:S(2)}, u32[]{:S(2)}) collective-permute-start(bf16[2,12,12,512]{3,0,2,1:T(2,128)(2,1)S(1)} %get-tuple-element.369), channel_id=1, source_target_pairs={{0,64},{64,128},{128,192},{192,256},{256,320},{320,384},{384,448},... | collective-permute-start | bytes 884744 | tf_op jit(solution)/shard_map/while/body/eval_jaxpr/ppermute | solution.py:24
  346.8 23.1 %copy-start.2 = (f32[1,512]{1,0:T(1,128)S(1)}, f32[1,512]{1,0:T(1,128)}, u32[]{:S(2)}) copy-start(f32[1,512]{1,0:T(1,128)} %get-tuple-element.412) | copy-start | bytes 6148 | tf_op jit(solution)/shard_map/while
  348.0 11.4 %collective-permute-start = (bf16[2,12,12,512]{3,0,2,1:T(2,128)(2,1)S(1)}, bf16[2,12,12,512]{3,0,2,1:T(2,128)(2,1)S(1)}, u32[]{:S(2)}, u32[]{:S(2)}) collective-permute-start(bf16[2,12,12,512]{3,0,2,1:T(2,128)(2,1)S(1)} %dynamic-slice_bitcast_fusion.2), channel_id=1, source_target_pairs={{0,320},{64,384},{128,448},{1,321},{65,385},{129,449},{2,322},{66,... | collective-permute-start | bytes 884744 | tf_op jit(solution)/shard_map/while/body/eval_jaxpr/ppermute | solution.py:24
  360.9 9.5 %copy-start.3 = (bf16[512,1536]{1,0:T(8,128)(2,1)S(1)}, bf16[512,1536]{1,0:T(8,128)(2,1)}, u32[]{:S(2)}) copy-start(bf16[512,1536]{1,0:T(8,128)(2,1)} %get-tuple-element.413) | copy-start | bytes 4718596 | tf_op jit(solution)/shard_map/while
  361.2 7.5 %collective-permute-start.1 = (bf16[2,12,6,512]{3,0,2,1:T(2,128)(2,1)S(1)}, bf16[2,12,6,512]{3,0,2,1:T(2,128)(2,1)S(1)}, u32[]{:S(2)}, u32[]{:S(2)}) collective-permute-start(bf16[2,12,6,512]{3,0,2,1:T(2,128)(2,1)S(1)} %get-tuple-element.358), channel_id=1, source_target_pairs={{1,0},{2,1},{3,2},{4,3},{5,4},{6,5},{7,6},{8,7},{9,8},{10,9},{11,1... | collective-permute-start | bytes 442376 | tf_op jit(solution)/shard_map/while/body/eval_jaxpr/ppermute | solution.py:18
  381.2 10.2 %collective-permute-start.2 = (bf16[2,12,6,512]{3,0,2,1:T(2,128)(2,1)S(1)}, bf16[2,12,6,512]{3,0,2,1:T(2,128)(2,1)S(1)}, u32[]{:S(2)}, u32[]{:S(2)}) collective-permute-start(bf16[2,12,6,512]{3,0,2,1:T(2,128)(2,1)S(1)} %get-tuple-element.368), channel_id=1, source_target_pairs={{63,0},{0,1},{1,2},{2,3},{3,4},{4,5},{5,6},{6,7},{7,8},{8,9},{9,10... | collective-permute-start | bytes 442376 | tf_op jit(solution)/shard_map/while/body/eval_jaxpr/ppermute | solution.py:18
  393.7 8.8 %collective-permute-start.3 = (bf16[2,12,12,512]{3,0,2,1:T(2,128)(2,1)S(1)}, bf16[2,12,12,512]{3,0,2,1:T(2,128)(2,1)S(1)}, u32[]{:S(2)}, u32[]{:S(2)}) collective-permute-start(bf16[2,12,12,512]{3,0,2,1:T(2,128)(2,1)S(1)} %get-tuple-element.369), channel_id=1, source_target_pairs={{0,64},{64,128},{128,192},{192,256},{256,320},{320,384},{384,448},... | collective-permute-start | bytes 884744 | tf_op jit(solution)/shard_map/while/body/eval_jaxpr/ppermute | solution.py:24
  402.5 23.1 %copy-start.2 = (f32[1,512]{1,0:T(1,128)S(1)}, f32[1,512]{1,0:T(1,128)}, u32[]{:S(2)}) copy-start(f32[1,512]{1,0:T(1,128)} %get-tuple-element.412) | copy-start | bytes 6148 | tf_op jit(solution)/shard_map/while
  403.7 11.4 %collective-permute-start = (bf16[2,12,12,512]{3,0,2,1:T(2,128)(2,1)S(1)}, bf16[2,12,12,512]{3,0,2,1:T(2,128)(2,1)S(1)}, u32[]{:S(2)}, u32[]{:S(2)}) collective-permute-start(bf16[2,12,12,512]{3,0,2,1:T(2,128)(2,1)S(1)} %dynamic-slice_bitcast_fusion.2), channel_id=1, source_target_pairs={{0,320},{64,384},{128,448},{1,321},{65,385},{129,449},{2,322},{66,... | collective-permute-start | bytes 884744 | tf_op jit(solution)/shard_map/while/body/eval_jaxpr/ppermute | solution.py:24
  416.7 9.5 %copy-start.3 = (bf16[512,1536]{1,0:T(8,128)(2,1)S(1)}, bf16[512,1536]{1,0:T(8,128)(2,1)}, u32[]{:S(2)}) copy-start(bf16[512,1536]{1,0:T(8,128)(2,1)} %get-tuple-element.413) | copy-start | bytes 4718596 | tf_op jit(solution)/shard_map/while
  416.9 7.5 %collective-permute-start.1 = (bf16[2,12,6,512]{3,0,2,1:T(2,128)(2,1)S(1)}, bf16[2,12,6,512]{3,0,2,1:T(2,128)(2,1)S(1)}, u32[]{:S(2)}, u32[]{:S(2)}) collective-permute-start(bf16[2,12,6,512]{3,0,2,1:T(2,128)(2,1)S(1)} %get-tuple-element.358), channel_id=1, source_target_pairs={{1,0},{2,1},{3,2},{4,3},{5,4},{6,5},{7,6},{8,7},{9,8},{10,9},{11,1... | collective-permute-start | bytes 442376 | tf_op jit(solution)/shard_map/while/body/eval_jaxpr/ppermute | solution.py:18
  436.9 10.2 %collective-permute-start.2 = (bf16[2,12,6,512]{3,0,2,1:T(2,128)(2,1)S(1)}, bf16[2,12,6,512]{3,0,2,1:T(2,128)(2,1)S(1)}, u32[]{:S(2)}, u32[]{:S(2)}) collective-permute-start(bf16[2,12,6,512]{3,0,2,1:T(2,128)(2,1)S(1)} %get-tuple-element.368), channel_id=1, source_target_pairs={{63,0},{0,1},{1,2},{2,3},{3,4},{4,5},{5,6},{6,7},{7,8},{8,9},{9,10... | collective-permute-start | bytes 442376 | tf_op jit(solution)/shard_map/while/body/eval_jaxpr/ppermute | solution.py:18
  449.5 8.8 %collective-permute-start.3 = (bf16[2,12,12,512]{3,0,2,1:T(2,128)(2,1)S(1)}, bf16[2,12,12,512]{3,0,2,1:T(2,128)(2,1)S(1)}, u32[]{:S(2)}, u32[]{:S(2)}) collective-permute-start(bf16[2,12,12,512]{3,0,2,1:T(2,128)(2,1)S(1)} %get-tuple-element.369), channel_id=1, source_target_pairs={{0,64},{64,128},{128,192},{192,256},{256,320},{320,384},{384,448},... | collective-permute-start | bytes 884744 | tf_op jit(solution)/shard_map/while/body/eval_jaxpr/ppermute | solution.py:24
  458.2 23.1 %copy-start.2 = (f32[1,512]{1,0:T(1,128)S(1)}, f32[1,512]{1,0:T(1,128)}, u32[]{:S(2)}) copy-start(f32[1,512]{1,0:T(1,128)} %get-tuple-element.412) | copy-start | bytes 6148 | tf_op jit(solution)/shard_map/while
  459.4 11.4 %collective-permute-start = (bf16[2,12,12,512]{3,0,2,1:T(2,128)(2,1)S(1)}, bf16[2,12,12,512]{3,0,2,1:T(2,128)(2,1)S(1)}, u32[]{:S(2)}, u32[]{:S(2)}) collective-permute-start(bf16[2,12,12,512]{3,0,2,1:T(2,128)(2,1)S(1)} %dynamic-slice_bitcast_fusion.2), channel_id=1, source_target_pairs={{0,320},{64,384},{128,448},{1,321},{65,385},{129,449},{2,322},{66,... | collective-permute-start | bytes 884744 | tf_op jit(solution)/shard_map/while/body/eval_jaxpr/ppermute | solution.py:24
  472.4 9.5 %copy-start.3 = (bf16[512,1536]{1,0:T(8,128)(2,1)S(1)}, bf16[512,1536]{1,0:T(8,128)(2,1)}, u32[]{:S(2)}) copy-start(bf16[512,1536]{1,0:T(8,128)(2,1)} %get-tuple-element.413) | copy-start | bytes 4718596 | tf_op jit(solution)/shard_map/while
  472.6 7.5 %collective-permute-start.1 = (bf16[2,12,6,512]{3,0,2,1:T(2,128)(2,1)S(1)}, bf16[2,12,6,512]{3,0,2,1:T(2,128)(2,1)S(1)}, u32[]{:S(2)}, u32[]{:S(2)}) collective-permute-start(bf16[2,12,6,512]{3,0,2,1:T(2,128)(2,1)S(1)} %get-tuple-element.358), channel_id=1, source_target_pairs={{1,0},{2,1},{3,2},{4,3},{5,4},{6,5},{7,6},{8,7},{9,8},{10,9},{11,1... | collective-permute-start | bytes 442376 | tf_op jit(solution)/shard_map/while/body/eval_jaxpr/ppermute | solution.py:18
  492.7 10.2 %collective-permute-start.2 = (bf16[2,12,6,512]{3,0,2,1:T(2,128)(2,1)S(1)}, bf16[2,12,6,512]{3,0,2,1:T(2,128)(2,1)S(1)}, u32[]{:S(2)}, u32[]{:S(2)}) collective-permute-start(bf16[2,12,6,512]{3,0,2,1:T(2,128)(2,1)S(1)} %get-tuple-element.368), channel_id=1, source_target_pairs={{63,0},{0,1},{1,2},{2,3},{3,4},{4,5},{5,6},{6,7},{7,8},{8,9},{9,10... | collective-permute-start | bytes 442376 | tf_op jit(solution)/shard_map/while/body/eval_jaxpr/ppermute | solution.py:18
  505.2 8.8 %collective-permute-start.3 = (bf16[2,12,12,512]{3,0,2,1:T(2,128)(2,1)S(1)}, bf16[2,12,12,512]{3,0,2,1:T(2,128)(2,1)S(1)}, u32[]{:S(2)}, u32[]{:S(2)}) collective-permute-start(bf16[2,12,12,512]{3,0,2,1:T(2,128)(2,1)S(1)} %get-tuple-element.369), channel_id=1, source_target_pairs={{0,64},{64,128},{128,192},{192,256},{256,320},{320,384},{384,448},... | collective-permute-start | bytes 884744 | tf_op jit(solution)/shard_map/while/body/eval_jaxpr/ppermute | solution.py:24
  514.0 23.1 %copy-start.2 = (f32[1,512]{1,0:T(1,128)S(1)}, f32[1,512]{1,0:T(1,128)}, u32[]{:S(2)}) copy-start(f32[1,512]{1,0:T(1,128)} %get-tuple-element.412) | copy-start | bytes 6148 | tf_op jit(solution)/shard_map/while
  515.2 11.4 %collective-permute-start = (bf16[2,12,12,512]{3,0,2,1:T(2,128)(2,1)S(1)}, bf16[2,12,12,512]{3,0,2,1:T(2,128)(2,1)S(1)}, u32[]{:S(2)}, u32[]{:S(2)}) collective-permute-start(bf16[2,12,12,512]{3,0,2,1:T(2,128)(2,1)S(1)} %dynamic-slice_bitcast_fusion.2), channel_id=1, source_target_pairs={{0,320},{64,384},{128,448},{1,321},{65,385},{129,449},{2,322},{66,... | collective-permute-start | bytes 884744 | tf_op jit(solution)/shard_map/while/body/eval_jaxpr/ppermute | solution.py:24
  528.1 9.5 %copy-start.3 = (bf16[512,1536]{1,0:T(8,128)(2,1)S(1)}, bf16[512,1536]{1,0:T(8,128)(2,1)}, u32[]{:S(2)}) copy-start(bf16[512,1536]{1,0:T(8,128)(2,1)} %get-tuple-element.413) | copy-start | bytes 4718596 | tf_op jit(solution)/shard_map/while
  528.3 7.5 %collective-permute-start.1 = (bf16[2,12,6,512]{3,0,2,1:T(2,128)(2,1)S(1)}, bf16[2,12,6,512]{3,0,2,1:T(2,128)(2,1)S(1)}, u32[]{:S(2)}, u32[]{:S(2)}) collective-permute-start(bf16[2,12,6,512]{3,0,2,1:T(2,128)(2,1)S(1)} %get-tuple-element.358), channel_id=1, source_target_pairs={{1,0},{2,1},{3,2},{4,3},{5,4},{6,5},{7,6},{8,7},{9,8},{10,9},{11,1... | collective-permute-start | bytes 442376 | tf_op jit(solution)/shard_map/while/body/eval_jaxpr/ppermute | solution.py:18
  548.4 10.2 %collective-permute-start.2 = (bf16[2,12,6,512]{3,0,2,1:T(2,128)(2,1)S(1)}, bf16[2,12,6,512]{3,0,2,1:T(2,128)(2,1)S(1)}, u32[]{:S(2)}, u32[]{:S(2)}) collective-permute-start(bf16[2,12,6,512]{3,0,2,1:T(2,128)(2,1)S(1)} %get-tuple-element.368), channel_id=1, source_target_pairs={{63,0},{0,1},{1,2},{2,3},{3,4},{4,5},{5,6},{6,7},{7,8},{8,9},{9,10... | collective-permute-start | bytes 442376 | tf_op jit(solution)/shard_map/while/body/eval_jaxpr/ppermute | solution.py:18
  560.9 8.8 %collective-permute-start.3 = (bf16[2,12,12,512]{3,0,2,1:T(2,128)(2,1)S(1)}, bf16[2,12,12,512]{3,0,2,1:T(2,128)(2,1)S(1)}, u32[]{:S(2)}, u32[]{:S(2)}) collective-permute-start(bf16[2,12,12,512]{3,0,2,1:T(2,128)(2,1)S(1)} %get-tuple-element.369), channel_id=1, source_target_pairs={{0,64},{64,128},{128,192},{192,256},{256,320},{320,384},{384,448},... | collective-permute-start | bytes 884744 | tf_op jit(solution)/shard_map/while/body/eval_jaxpr/ppermute | solution.py:24
  (8 other events, 8.4 us)
Sparse Core Ops, SparseCore 0:
  572.0 89.4 all-reduce.1
where the time goes:
time: 674 us; the launch traced here: 671 us
  waiting for transfers between devices  285 us (42%)
  starting transfers between devices  188 us (28%)
  other arithmetic  82.1 us (12%)
  local copies, waits for them, and re-layouts  79.8 us (12%)
  matrix products  20.2 us (3%)
  between operations  13.4 us (2%)
    ppermute x20, starting transfers between devices, passed_along(): return lax.ppermute(value, axis, pairs)  117 us
    ppermute x20, waiting for transfers between devices, from_behind(): return lax.ppermute(block, axis, route)  110 us
    psum x1, waiting for transfers between devices, from_root(): return lax.psum(kept, axis)  89.6 us
    ppermute x20, waiting for transfers between devices, passed_along(): return lax.ppermute(value, axis, pairs)  86 us
    ppermute x20, starting transfers between devices, from_behind(): return lax.ppermute(block, axis, route)  71.2 us
    while x90, local copies, waits for them, and re-layouts  24.8 us
    sub x10, other arithmetic, attend(): scores = scores - jnp.max(scores, axis=-1, keepdims=True)  23.5 us
    select_n x10, other arithmetic, keep(): return jnp.where(live, kept, saved)  22.8 us
  transfers between devices with their start and end apart: 41, of which 41 were waited for; matrix products, arithmetic and copies ran while one was open for 0% of the time, Pallas kernels for 0%

commit v1 on v0

v1 whole, which is shorter than its diff:
```python
import functools

import jax
import jax.numpy as jnp
from jax import lax
from jax.experimental import pallas as pl
from jax.experimental.pallas import tpu as pltpu
from jax.sharding import PartitionSpec as P

MESH = pl.DeviceIdType.MESH
F32, BF16 = jnp.float32, jnp.bfloat16
HEADS = 8
HALF = 72
PAD = 80
WIN = 2 * HALF
EPS = 1e-05
LAYERS = 8
SKIP = 5
LANES = 128


def dot(a, b):
    return jnp.dot(a, b, preferred_element_type=F32)


def dot_t(a, b):
    return lax.dot_general(a, b, (((1,), (1,)), ((), ())), preferred_element_type=F32)


def normalize(x, gain):
    mean = jnp.mean(x, axis=-1, keepdims=True)
    centred = x - mean
    spread = jnp.mean(centred * centred, axis=-1, keepdims=True)
    return (centred * lax.rsqrt(spread + EPS) * gain).astype(BF16)


def attend(query, kv, width):
    rows = query.shape[0]
    low = lax.broadcasted_iota(jnp.int32, (rows, LANES), 1) < LANES // 2
    mixed = []
    for pair in range(width // LANES):
        cols = slice(pair * LANES, (pair + 1) * LANES)
        q = query[:, cols]
        both = jnp.concatenate([jnp.where(low, q, 0.0), jnp.where(low, 0.0, q)], 0).astype(BF16)
        scores = dot_t(both, kv[:, cols])
        top = jnp.max(scores, axis=-1, keepdims=True)
        weights = jnp.exp2(scores - top).astype(BF16)
        values = kv[:, width + pair * LANES : width + (pair + 1) * LANES]
        summed = dot(weights, jnp.concatenate([values, jnp.ones_like(values)], 1))
        summed = summed[:, :LANES] / summed[:, LANES:]
        mixed.append(jnp.where(low, summed[:rows], summed[rows:]))
    return jnp.concatenate(mixed, 1).astype(BF16)


def swizzled(lon, lons):
    high, low = lon // (lons // 2), lax.rem(lon, 2)
    swapped = high + low - 2 * high * low
    return lax.rem(lon, lons // 2) + swapped * (lons // 2)


def kernel(micro, x_ref, gain_ref, wqkv_ref, wout_ref, whead_ref, out_ref,
           xin, gain, wqkv, wout, whead, xs, kv, arrived, skips, sent, outs, outs_in, halves, joined,
           load_sem, arrive_sem, send_sem, skip_sem, skipsend_sem, head_sem, headsend_sem, out_sem, outsend_sem):
    sections, lons = lax.axis_size("section"), lax.axis_size("lon")
    sec, lon = lax.axis_index("section"), lax.axis_index("lon")
    odd = lax.rem(sec, 2)
    width = wout_ref.shape[-1]
    streams = 2 * micro
    last = sections - 1
    mine = jnp.where(odd == 1, swizzled(lon, lons), lon)

    def holder(section, block):
        block = lax.rem(block + lons, lons)
        return section, jnp.where(lax.rem(section, 2) == 1, swizzled(block, lons), block)

    def target(half, to):
        return holder(to, mine + half - 1 + odd)

    loads = [
        pltpu.make_async_copy(gain_ref, gain, load_sem.at[0]),
        pltpu.make_async_copy(wqkv_ref.at[0], wqkv, load_sem.at[1]),
        pltpu.make_async_copy(wout_ref.at[0], wout, load_sem.at[2]),
        pltpu.make_async_copy(whead_ref, whead.at[sec], load_sem.at[3]),
    ]
    for load in loads:
        load.start()
    load_x = pltpu.make_async_copy(x_ref, xin, load_sem.at[4])
    pl.when(sec == 0)(load_x.start)

    barrier = pltpu.get_barrier_semaphore()

    def greet(where):
        pl.semaphore_signal(barrier, inc=1, device_id=where, device_id_type=MESH)

    def greet_sources(behind):
        before = sec - behind
        was_odd = lax.rem(before, 2)
        for half in range(2):
            greet(holder(before, mine - (half - 1 + was_odd)))

    pl.when(sec > 0)(lambda: greet_sources(1))
    pl.when(sec >= SKIP)(lambda: greet_sources(SKIP))

    @pl.when(sec == last)
    def _():
        for c in range(last):
            greet((c, lon))

    def out_source(half):
        return holder(last, lon - half)

    for half in range(2):
        where = out_source(half)
        here = jnp.logical_and(sec == last, where[1] == lon)
        pl.when(jnp.logical_not(here))(functools.partial(greet, where))

    itself = jnp.logical_and(sec == last, mine == lon)
    itself_next = jnp.logical_and(sec == last, lax.rem(mine + 1, lons) == lon)
    count = jnp.where(sec < last, 3, 2 * sections)
    count = count + jnp.where(sec < LAYERS - SKIP, 2, 0)
    count = count - jnp.where(itself, 1, 0) - jnp.where(itself_next, 1, 0)
    pl.semaphore_wait(barrier, count)

    head_copy = pltpu.make_async_remote_copy(
        src_ref=whead.at[sec], dst_ref=whead.at[sec], send_sem=headsend_sem, recv_sem=head_sem.at[sec],
        device_id=(last, lon), device_id_type=MESH)
    for load in loads:
        load.wait()

    pl.when(jnp.logical_and(sec >= 3, sec < last))(head_copy.start)
    pl.when(sec == 0)(load_x.wait)

    def step_copy(stream, half):
        return pltpu.make_async_remote_copy(
            src_ref=sent.at[stream, half], dst_ref=arrived.at[stream, 1 - half],
            send_sem=send_sem.at[stream, half], recv_sem=arrive_sem.at[stream, 1 - half],
            device_id=target(half, jnp.minimum(sec + 1, last)), device_id_type=MESH)

    def skip_copy(stream, half):
        return pltpu.make_async_remote_copy(
            src_ref=sent.at[stream, half], dst_ref=skips.at[stream, 1 - half],
            send_sem=skipsend_sem.at[stream, half], recv_sem=skip_sem.at[stream, 1 - half],
            device_id=target(half, jnp.minimum(sec + SKIP, last)), device_id_type=MESH)

    def out_copy(stream, half, c):
        return pltpu.make_async_remote_copy(
            src_ref=outs.at[stream, half, c], dst_ref=outs_in.at[stream, 1 - half],
            send_sem=outsend_sem.at[stream, half, c], recv_sem=out_sem.at[stream, 1 - half],
            device_id=(c, lax.rem(mine + half, lons)), device_id_type=MESH)

    def out_local(stream, half, c):
        return pltpu.make_async_copy(outs.at[stream, half, c], outs_in.at[stream, 1 - half], out_sem.at[stream, 1 - half])

    stays = (itself, itself_next)

    def step(stream, carry):
        @pl.when(sec == 0)
        def _():
            m, lat = stream // 2, lax.rem(stream, 2)
            for level in range(2):
                for a in range(6):
                    block = xin[m, level, lat * 6 + a].astype(F32)
                    at = (level * 6 + a) * 6
                    xs[at : at + 6] = block[:6]
                    xs[HALF + at : HALF + at + 6] = block[6:]

        @pl.when(sec > 0)
        def _():
            for half in range(2):
                step_copy(stream, 1 - half).wait_recv()

        @pl.when(jnp.logical_and(sec > 0, sec < SKIP))
        def _():
            for half in range(2):
                xs[half * HALF : (half + 1) * HALF] = arrived[stream, half].astype(F32)[:HALF]

        @pl.when(sec >= SKIP)
        def _():
            for half in range(2):
                skip_copy(stream, 1 - half).wait_recv()
                joined_up = arrived[stream, half].astype(F32) + skips[stream, half].astype(F32)
                xs[half * HALF : (half + 1) * HALF] = joined_up.astype(BF16).astype(F32)[:HALF]

        x = xs[...]
        normed = normalize(x, gain[...])
        query = dot(normed, wqkv[:, :width]) * ((width // HEADS) ** -0.5 * 1.4426950408889634)
        kv[...] = dot(normed, wqkv[:, width:]).astype(BF16)
        y = x + dot(attend(query, kv, width), wout[...])
        filler = jnp.zeros((PAD - HALF, width), F32)
        for half in range(2):
            sent[stream, half] = jnp.concatenate([y[half * HALF : (half + 1) * HALF], filler], 0).astype(BF16)

        @pl.when(sec < last)
        def _():
            for half in range(2):
                step_copy(stream, half).start()

        @pl.when(sec == last)
        def _():
            @pl.when(stream == 0)
            def _():
                for c in range(last):
                    pltpu.make_async_copy(whead.at[c], whead.at[c], head_sem.at[c]).wait()

            both = jnp.concatenate([y, jnp.zeros((2 * (PAD - HALF), width), F32)], 0).astype(BF16)
            for pair in range(sections // 2):
                cols = jnp.concatenate([whead[2 * pair], whead[2 * pair + 1]], 1)
                made = dot(both, cols)
                for side in range(2):
                    piece = made[:, side * LANES : (side + 1) * LANES]
                    for half in range(2):
                        rows = piece[half * HALF : half * HALF + PAD]
                        outs[stream, half, 2 * pair + side] = rows.astype(BF16)
                        c = 2 * pair + side
                        if c < last:
                            out_copy(stream, half, c).start()
                        else:
                            pl.when(jnp.logical_not(stays[half]))(out_copy(stream, half, c).start)
                            pl.when(stays[half])(out_local(stream, half, c).start)

        return carry

    lax.fori_loop(0, streams, step, 0)

    @pl.when(sec < LAYERS - SKIP)
    def _():
        def send_skips(stream, carry):
            for half in range(2):
                skip_copy(stream, half).start()
            return carry

        lax.fori_loop(0, streams, send_skips, 0)

    pl.when(sec < 3)(head_copy.start)

    def collect(stream, carry):
        m, lat = stream // 2, lax.rem(stream, 2)
        for half in range(2):
            out_copy(stream, 1 - half, 0).wait_recv()
            halves[half] = outs_in[stream, half].astype(F32)
        for half in range(2):
            for g in range(12):
                joined[g, half * 6 : half * 6 + 6] = halves[half, g * 6 : g * 6 + 6]
        for level in range(2):
            out_ref[m, level, pl.ds(lat * 6, 6)] = joined[level * 6 : level * 6 + 6].astype(BF16)
        return carry

    lax.fori_loop(0, streams, collect, 0)

    def sent_all(stream, carry):
        @pl.when(sec < last)
        def _():
            for half in range(2):
                step_copy(stream, half).wait_send()

        @pl.when(sec < LAYERS - SKIP)
        def _():
            for half in range(2):
                skip_copy(stream, half).wait_send()

        @pl.when(sec == last)
        def _():
            for half in range(2):
                for c in range(sections):
                    if c < last:
                        out_copy(stream, half, c).wait_send()
                    else:
                        pl.when(jnp.logical_not(stays[half]))(out_copy(stream, half, c).wait_send)

        return carry

    lax.fori_loop(0, streams, sent_all, 0)
    pl.when(sec < last)(head_copy.wait_send)


def per_device(inputs, norm_gain, w_qkv, w_out, w_head):
    micro, levels, lat, lon, width = inputs.shape
    sections = lax.axis_size("section")
    columns = w_head.shape[1]
    streams = 2 * micro
    dma = pltpu.SemaphoreType.DMA
    hbm = pl.BlockSpec(memory_space=pl.ANY)
    vmem = pl.BlockSpec(memory_space=pltpu.VMEM)
    return pl.pallas_call(
        functools.partial(kernel, micro),
        out_shape=jax.ShapeDtypeStruct((micro, levels, lat, lon, columns), BF16),
        in_specs=[hbm] * 5,
        out_specs=vmem,
        scratch_shapes=[
            pltpu.VMEM(inputs.shape, BF16),
            pltpu.VMEM(norm_gain.shape, F32),
            pltpu.VMEM(w_qkv.shape[1:], BF16),
            pltpu.VMEM(w_out.shape[1:], BF16),
            pltpu.VMEM((sections,) + w_head.shape, BF16),
            pltpu.VMEM((WIN, width), F32),
            pltpu.VMEM((WIN, 2 * width), BF16),
            pltpu.VMEM((streams, 2, PAD, width), BF16),
            pltpu.VMEM((streams, 2, PAD, width), BF16),
            pltpu.VMEM((streams, 2, PAD, width), BF16),
            pltpu.VMEM((streams, 2, sections, PAD, columns), BF16),
            pltpu.VMEM((streams, 2, PAD, columns), BF16),
            pltpu.VMEM((2, PAD, columns), F32),
            pltpu.VMEM((12, 12, columns), F32),
            dma((5,)),
            dma((streams, 2)),
            dma((streams, 2)),
            dma((streams, 2)),
            dma((streams, 2)),
            dma((sections,)),
            dma,
            dma((streams, 2)),
            dma((streams, 2, sections)),
        ],
        compiler_params=pltpu.CompilerParams(
            collective_id=0, has_side_effects=True, vmem_limit_bytes=40 * 2**20
        ),
    )(inputs, norm_gain, w_qkv, w_out, w_head)


def solution(mesh):
    placed = (
        P(None, None, None, "lon", None),
        P("section", None),
        P("section", None, None),
        P("section", None, None),
        P(None, "section"),
    )
    return jax.shard_map(
        per_device,
        mesh=mesh,
        in_specs=placed,
        out_specs=P(None, None, None, "lon", "section"),
        check_vma=False,
    )
```

time: 674 us -> 104 us (0.15)
  the two profiles are of different devices: /device:TPU:4 before, /device:TPU:5 now
where the time goes in v1:
time: 104 us
  Pallas kernels  100 us (96%)
  local copies, waits for them, and re-layouts  3.69 us (4%)
    pallas_call x1, Pallas kernels, per_device(): pl.pallas_call(functools.partial(kernel, micro), out_shape=jax.ShapeDtype...  100 us
    unnamed x9, local copies, waits for them, and re-layouts  2.78 us

profile of v1, /device:TPU:5, one launch (start us, length us, event | category | flops | bytes accessed | tf_op | source)
XLA Modules:
  0.0 104.0 jit_solution(17825106009809581373)
XLA Ops:
  0.0 0.0 copy-start.2
  0.0 0.0 copy-start
  0.0 0.0 copy-start.3
  0.0 1.5 %copy.6.x_ref = bf16[3,2,12,12,512]{4,3,2,1,0:T(8,128)(2,1)S(1)} copy(bf16[3,2,12,12,512]{4,1,3,2,0:T(2,128)(2,1)} %param.5) | data formatting | bytes 1769472 | tf_op args[0]
  1.5 0.0 copy-done.2
  1.6 0.2 copy-done
  1.8 0.0 copy-done.3
  1.8 0.0 copy-start.1
  1.8 1.0 copy-done.1
  2.8 100.3 %shard_map.55 = bf16[3,2,12,12,128]{4,3,2,1,0:T(8,128)(2,1)S(1)} custom-call(bf16[3,2,12,12,512]{4,3,2,1,0:T(8,128)(2,1)S(1)} %copy.6.x_ref, f32[1,512]{1,0:T(1,128)S(1)} %copy-done.3, bf16[1,512,1536]{2,1,0:T(8,128)(2,1)S(1)} %copy-done, bf16[1,512,512]{2,1,0:T(8,128)(2,1)S(1)} %copy-done.1, bf16[512,128]{1,0:T(8,128)(2,1)S(1)} %copy-done.2), custom_call_target="tpu_custom_call" | custom-call | tf_op jit(solution)/shard_map/pallas_call | solution.py:284
  103.1 0.9 copy.7
Async XLA Ops:
  0.0 1.5 %copy-start.2 = (bf16[512,128]{1,0:T(8,128)(2,1)S(1)}, bf16[512,128]{1,0:T(8,128)(2,1)}, u32[]{:S(2)}) copy-start(bf16[512,128]{1,0:T(8,128)(2,1)} %whead_ref.1) | copy-start | bytes 393220
  0.0 1.7 %copy-start = (bf16[1,512,1536]{2,1,0:T(8,128)(2,1)S(1)}, bf16[1,512,1536]{2,1,0:T(8,128)(2,1)}, u32[]{:S(2)}) copy-start(bf16[1,512,1536]{2,1,0:T(8,128)(2,1)} %wqkv_ref.1) | copy-start | bytes 4718596
  0.0 1.8 %copy-start.3 = (f32[1,512]{1,0:T(1,128)S(1)}, f32[1,512]{1,0:T(1,128)}, u32[]{:S(2)}) copy-start(f32[1,512]{1,0:T(1,128)} %gain_ref.1) | copy-start | bytes 6148
  1.8 1.0 %copy-start.1 = (bf16[1,512,512]{2,1,0:T(8,128)(2,1)S(1)}, bf16[1,512,512]{2,1,0:T(8,128)(2,1)}, u32[]{:S(2)}) copy-start(bf16[1,512,512]{2,1,0:T(8,128)(2,1)} %wout_ref.1) | copy-start | bytes 1572868

commit v2 on v1

v2 whole, which is shorter than its diff:
```python
import functools

import jax
import jax.numpy as jnp
from jax import lax
from jax.experimental import pallas as pl
from jax.experimental.pallas import tpu as pltpu
from jax.sharding import PartitionSpec as P

MESH = pl.DeviceIdType.MESH
F32, BF16 = jnp.float32, jnp.bfloat16
HEADS = 8
AHEAD = 3
HALF = 72
WIN = 2 * HALF
EPS = 1e-05
LAYERS = 8
SKIP = 5
LAG = 1
LANES = 128


def dot(a, b):
    return jnp.dot(a, b, preferred_element_type=F32)


def dot_t(a, b):
    return lax.dot_general(a, b, (((1,), (1,)), ((), ())), preferred_element_type=F32)


def normalize(x, gain):
    mean = jnp.mean(x, axis=-1, keepdims=True)
    centred = x - mean
    spread = jnp.mean(centred * centred, axis=-1, keepdims=True)
    return (centred * lax.rsqrt(spread + EPS) * gain).astype(BF16)


def attend(query, kv, width):
    rows = query.shape[0]
    low = lax.broadcasted_iota(jnp.int32, (rows, LANES), 1) < LANES // 2
    mixed = []
    for pair in range(width // LANES):
        cols = slice(pair * LANES, (pair + 1) * LANES)
        q = query[:, cols]
        both = jnp.concatenate([jnp.where(low, q, 0.0), jnp.where(low, 0.0, q)], 0).astype(BF16)
        scores = dot_t(both, kv[:, cols])
        top = jnp.max(scores, axis=-1, keepdims=True)
        weights = jnp.exp2(scores - top).astype(BF16)
        values = kv[:, width + pair * LANES : width + (pair + 1) * LANES]
        summed = dot(weights, jnp.concatenate([values, jnp.ones_like(values)], 1))
        summed = summed[:, :LANES] / summed[:, LANES:]
        mixed.append(jnp.where(low, summed[:rows], summed[rows:]))
    return jnp.concatenate(mixed, 1).astype(BF16)


def split(lon, lons):
    low = lax.rem(lon, 2)
    high = lon // (lons // 2)
    return high, lon - low - high * (lons // 2), low


def other(high, low):
    flip = 1 - low
    return high + flip - 2 * high * flip


def holder(layer, block, lons):
    block = lax.rem(block + lons, lons)
    high, middle, low = split(block, lons)
    first = (0, block)
    second = (1, other(high, low) * (lons // 2) + middle + low)
    later = (2 * (layer // 2) + low, block - low + lax.rem(layer, 2))
    return tuple(jnp.where(layer == 0, f, jnp.where(layer == 1, g, h)) for f, g, h in zip(first, second, later))


def role(sec, lon, lons):
    high, middle, low = split(lon, lons)
    side = lax.rem(sec, 2)
    layer = jnp.where(sec < 2, sec, sec - side + low)
    crossed = other(high, low) * (lons // 2) + middle + low
    block = jnp.where(sec == 0, lon, jnp.where(sec == 1, crossed, lon - low + side))
    return layer, block


def kernel(micro, x_ref, gain_ref, wqkv_ref, wout_ref, whead_ref, out_ref,
           xin, gain, wqkv, wout, whead, xs, kv, arrived, skips, relayed, sent, outs,
           load_sem, arrive_sem, send_sem, skip_sem, skipsend_sem, head_sem, headsend_sem, out_sem, outsend_sem,
           swap_sem, swapsend_sem, relay_sem, relaysend_sem):
    sections, lons = lax.axis_size("section"), lax.axis_size("lon")
    sec, lon = lax.axis_index("section"), lax.axis_index("lon")
    layer, mine = role(sec, lon, lons)
    odd = lax.rem(layer, 2)
    width = wout_ref.shape[-1]
    streams = 2 * micro
    last = LAYERS - 1
    core = lax.rem(lon, 2)
    side = lax.rem(sec, 2)
    swaps = jnp.logical_and(sec >= 2, side != core)
    keeps = jnp.logical_not(swaps)

    def target(half, to):
        return holder(to, mine + half - 1 + odd, lons)

    relays = sec >= sections - 2
    from_sec = sec - (sections - 2)
    from_layer, from_block = role(from_sec, lon, lons)

    partners = [(sec + 1 - 2 * side, lax.rem(lon + h * (lons // 2), lons) + 1 - 2 * core) for h in range(2)]

    load_head = pltpu.make_async_copy(whead_ref, whead.at[sec], load_sem.at[3])
    load_head.start()
    load_x = pltpu.make_async_copy(x_ref, xin, load_sem.at[4])
    pl.when(layer == 0)(load_x.start)
    loads = [
        pltpu.make_async_copy(gain_ref, gain, load_sem.at[0]),
        pltpu.make_async_copy(wqkv_ref.at[0], wqkv, load_sem.at[1]),
        pltpu.make_async_copy(wout_ref.at[0], wout, load_sem.at[2]),
    ]

    @pl.when(keeps)
    def _():
        for load in loads:
            load.start()

    barrier = pltpu.get_barrier_semaphore()

    def greet(where):
        pl.semaphore_signal(barrier, inc=1, device_id=where, device_id_type=MESH)

    def source(behind, half):
        before = layer - behind
        return holder(before, mine - (half - 1 + lax.rem(before + LAYERS, 2)), lons)

    @pl.when(layer > 0)
    def _():
        for half in range(2):
            greet(source(1, half))

    @pl.when(layer >= SKIP)
    def _():
        for half in range(2):
            where = source(SKIP, half)
            greet((jnp.where(layer < last, where[0] + sections - 2, where[0]), where[1]))

    pl.when(relays)(lambda: greet((from_sec, lon)))

    @pl.when(swaps)
    def _():
        for where in partners:
            greet(where)

    for half in range(2):
        where = holder(jnp.int32(last), lon - half, lons)
        here = jnp.logical_and(where[0] == sec, where[1] == lon)
        pl.when(jnp.logical_not(here))(functools.partial(greet, where))

    @pl.when(layer == last)
    def _():
        for c in range(sections):
            pl.when(sec != c)(functools.partial(greet, (c, lon)))

    @pl.when(layer == 0)
    def _():
        load_x.wait()

        def place(stream, carry):
            m, lat = stream // 2, lax.rem(stream, 2)
            for half in range(2):
                for a in range(6):
                    block = xin[m, lat * 6 + a, half * 6 : half * 6 + 6].astype(F32)
                    xs[a * 12 : a * 12 + 12] = block.reshape(12, width)
                arrived[stream, half] = xs[:HALF].astype(BF16)
            return carry

        lax.fori_loop(0, streams, place, 0)

    count = jnp.where(layer < last, 2, 2 * sections - 1)
    count = count + jnp.where(layer < 2, 1, jnp.where(layer < LAYERS - SKIP, 2, 0)) + jnp.where(swaps, 2, 0) + jnp.where(relays, 2, 0)
    count = count + jnp.where(core == 1, jnp.where(sec < sections - 2, 2, 1), 0)

    @pl.when(layer > 0)
    @jax.named_scope('greet')
    def _():
        pl.semaphore_wait(barrier, count)

    def swap_copy(half, piece):
        where = partners[half]
        rows = pl.ds(half * (width // 2), width // 2)
        src, dst = ((wqkv_ref.at[0, rows], wqkv.at[rows]), (wout_ref.at[0, rows], wout.at[rows]), (gain_ref, gain))[piece]
        return pltpu.make_async_remote_copy(
            src_ref=src, dst_ref=dst, send_sem=swapsend_sem.at[piece], recv_sem=swap_sem.at[piece],
            device_id=where, device_id_type=MESH)

    swap_list = ((0, 2), (0, 0), (1, 0), (0, 1), (1, 1))

    @pl.when(swaps)
    def _():
        for half, piece in swap_list:
            swap_copy(half, piece).start()

    def swap_wait(sems):
        for piece, ref in enumerate((wqkv, wout, gain)):
            pltpu.make_async_copy(ref, ref, sems.at[piece]).wait()

    def head_copy(b):
        return pltpu.make_async_remote_copy(
            src_ref=whead.at[sec], dst_ref=whead.at[sec], send_sem=headsend_sem.at[b], recv_sem=head_sem,
            device_id=(sections - 2 + b, lon), device_id_type=MESH)

    def each_head(act):
        @pl.when(core == 1)
        def _():
            for b in range(2):
                pl.when(sec != sections - 2 + b)(lambda: act(head_copy(b)))

    load_head.wait()

    @pl.when(keeps)
    def _():
        for load in loads:
            load.wait()

    def step_copy(stream, half):
        return pltpu.make_async_remote_copy(
            src_ref=sent.at[stream, half], dst_ref=arrived.at[stream, 1 - half],
            send_sem=send_sem, recv_sem=arrive_sem.at[stream, 1 - half],
            device_id=target(half, jnp.minimum(layer + 1, last)), device_id_type=MESH)

    def relay_in(stream, half):
        return pltpu.make_async_remote_copy(
            src_ref=sent.at[stream, half], dst_ref=relayed.at[stream, half],
            send_sem=skipsend_sem, recv_sem=relay_sem.at[stream, half],
            device_id=(lax.rem(sec + sections - 2, sections), lon), device_id_type=MESH)

    def relay_out(stream, half):
        return pltpu.make_async_remote_copy(
            src_ref=relayed.at[stream, half], dst_ref=skips.at[stream, 1 - half],
            send_sem=relaysend_sem, recv_sem=skip_sem.at[stream, 1 - half],
            device_id=holder(from_layer + SKIP, from_block + half - 1 + lax.rem(from_layer, 2), lons), device_id_type=MESH)

    def skip_copy(stream, half):
        return pltpu.make_async_remote_copy(
            src_ref=sent.at[stream, half], dst_ref=skips.at[stream, 1 - half],
            send_sem=skipsend_sem, recv_sem=skip_sem.at[stream, 1 - half],
            device_id=target(half, jnp.minimum(layer + SKIP, last)), device_id_type=MESH)

    @jax.named_scope('relay')
    def relay(stream):
        for half in range(2):
            relay_in(stream, half).wait_recv()
            relay_out(stream, half).start()

    def out_copy(stream, half, c):
        return pltpu.make_async_remote_copy(
            src_ref=outs.at[(stream * 2 + half) * sections + c], dst_ref=out_ref.at[stream, 1 - half],
            send_sem=outsend_sem, recv_sem=out_sem,
            device_id=(c, lax.rem(mine + half, lons)), device_id_type=MESH)

    def out_local(stream, half, c):
        return pltpu.make_async_copy(outs.at[(stream * 2 + half) * sections + c], out_ref.at[stream, 1 - half], out_sem)

    def stays(half, c):
        return jnp.logical_and(sec == c, lax.rem(mine + half, lons) == lon)

    def out_side(stream, to):
        def send(row, carry):
            c = 2 * row + to
            for half in range(2):
                pl.when(jnp.logical_not(stays(half, c)))(lambda: out_copy(stream, half, c).start())
                pl.when(stays(half, c))(lambda: out_local(stream, half, c).start())
            return carry

        lax.fori_loop(0, sections // 2, send, 0, unroll=True)

    pl.when(sec >= 4)(lambda: each_head(lambda c: c.start()))

    def relay_some(first, count):
        def one(stream, carry):
            relay(stream)
            return carry

        lax.fori_loop(first, count, one, 0)

    pl.when(sec == sections - 2)(lambda: relay_some(0, streams))
    pl.when(sec == sections - 1)(lambda: relay_some(0, AHEAD))

    def step(stream, carry):
        pl.when(jnp.logical_and(sec == sections - 1, stream < streams - AHEAD))(lambda: relay(stream + AHEAD))

        @pl.when(layer > 0)
        @jax.named_scope('arrive')
        def _():
            for half in range(2):
                step_copy(stream, 1 - half).wait_recv()

        @pl.when(layer < SKIP)
        def _():
            for half in range(2):
                xs[half * HALF : (half + 1) * HALF] = arrived[stream, half].astype(F32)

        @pl.when(layer >= SKIP)
        def _():
            for half in range(2):
                with jax.named_scope('skip'):
                    skip_copy(stream, 1 - half).wait_recv()
                joined = arrived[stream, half].astype(F32) + skips[stream, half].astype(F32)
                xs[half * HALF : (half + 1) * HALF] = joined.astype(BF16).astype(F32)

        first_swapped = jnp.logical_and(swaps, stream == 0)

        @pl.when(first_swapped)
        @jax.named_scope('swap')
        def _():
            swap_wait(swap_sem)

        scope = jax.named_scope('block')
        scope.__enter__()
        x = xs[...]
        normed = normalize(x, gain[...])
        query = dot(normed, wqkv[:, :width]) * ((width // HEADS) ** -0.5 * 1.4426950408889634)
        kv[...] = dot(normed, wqkv[:, width:]).astype(BF16)
        y = x + dot(attend(query, kv, width), wout[...])
        for half in range(2):
            sent[stream, half] = y[half * HALF : (half + 1) * HALF].astype(BF16)

        scope.__exit__(None, None, None)

        @pl.when(jnp.logical_and(layer == 0, stream == 0))
        @jax.named_scope('greet')
        def _():
            pl.semaphore_wait(barrier, count)

        @pl.when(layer < last)
        def _():
            for half in range(2):
                step_copy(stream, half).start()

        @pl.when(layer < 2)
        def _():
            for half in range(2):
                relay_in(stream, half).start()

        @pl.when(layer == 2)
        def _():
            for half in range(2):
                skip_copy(stream, half).start()

        @pl.when(layer == last)
        @jax.named_scope('head')
        def _():
            @pl.when(stream == 0)
            @jax.named_scope('headwait')
            def _():
                others = whead.at[pl.ds(0, sections - 1)]
                pltpu.make_async_copy(others, others, head_sem).wait()

            both = y.astype(BF16)
            for pair in range(sections // 2):
                cols = jnp.concatenate([whead[2 * pair], whead[2 * pair + 1]], 1)
                made = dot(both, cols)
                for part in range(2):
                    piece = made[:, part * LANES : (part + 1) * LANES]
                    for half in range(2):
                        rows = piece[half * HALF : (half + 1) * HALF]
                        outs[(stream * 2 + half) * sections + 2 * pair + part] = rows.astype(BF16)
            out_side(stream, side)
            pl.when(stream >= LAG)(lambda: out_side(stream - LAG, 1 - side))

        return carry

    lax.fori_loop(0, streams, step, 0)

    @pl.when(layer == last)
    def _():
        for late in range(LAG):
            out_side(streams - LAG + late, 1 - side)

    pl.when(sec < 4)(lambda: each_head(lambda c: c.start()))

    with jax.named_scope('output'):
        pltpu.make_async_copy(out_ref, out_ref, out_sem).wait()

    @pl.when(layer < last)
    def _():
        pltpu.make_async_copy(sent, sent, send_sem).wait()

    @pl.when(layer < LAYERS - SKIP)
    def _():
        pltpu.make_async_copy(sent, sent, skipsend_sem).wait()

    @pl.when(relays)
    def _():
        pltpu.make_async_copy(relayed, relayed, relaysend_sem).wait()

    @pl.when(layer == last)
    def _():
        most = outs.at[pl.ds(0, streams * (2 * sections - 1))]
        pltpu.make_async_copy(most, most, outsend_sem).wait()

    each_head(lambda c: c.wait_send())

    @pl.when(swaps)
    def _():
        swap_wait(swapsend_sem)


def per_device(inputs, norm_gain, w_qkv, w_out, w_head):
    inputs = inputs.transpose(0, 2, 3, 1, 4)
    micro, lat, lon, levels, width = inputs.shape
    sections = lax.axis_size("section")
    columns = w_head.shape[1]
    streams = 2 * micro
    dma = pltpu.SemaphoreType.DMA
    hbm = pl.BlockSpec(memory_space=pl.ANY)
    decoded = pl.pallas_call(
        functools.partial(kernel, micro),
        out_shape=jax.ShapeDtypeStruct((streams, 2, HALF, columns), BF16),
        in_specs=[hbm] * 5,
        out_specs=hbm,
        scratch_shapes=[
            pltpu.VMEM(inputs.shape, BF16),
            pltpu.VMEM(norm_gain.shape, F32),
            pltpu.VMEM(w_qkv.shape[1:], BF16),
            pltpu.VMEM(w_out.shape[1:], BF16),
            pltpu.VMEM((sections,) + w_head.shape, BF16),
            pltpu.VMEM((WIN, width), F32),
            pltpu.VMEM((WIN, 2 * width), BF16),
            pltpu.VMEM((streams, 2, HALF, width), BF16),
            pltpu.VMEM((streams, 2, HALF, width), BF16),
            pltpu.VMEM((streams, 2, HALF, width), BF16),
            pltpu.VMEM((streams, 2, HALF, width), BF16),
            pltpu.VMEM((streams * 2 * sections, HALF, columns), BF16),
            dma((5,)),
            dma((streams, 2)),
            dma,
            dma((streams, 2)),
            dma,
            dma,
            dma((2,)),
            dma,
            dma,
            dma((3,)),
            dma((3,)),
            dma((streams, 2)),
            dma,
        ],
        compiler_params=pltpu.CompilerParams(
            collective_id=0, has_side_effects=True, vmem_limit_bytes=60 * 2**20
        ),
    )(inputs, norm_gain, w_qkv, w_out, w_head)
    decoded = decoded.reshape(micro, 2, 2, lat // 2, lon // 2, levels, columns)
    return decoded.transpose(0, 5, 1, 3, 2, 4, 6).reshape(micro, levels, lat, lon, columns)


def solution(mesh):
    placed = (
        P(None, None, None, "lon", None),
        P("section", None),
        P("section", None, None),
        P("section", None, None),
        P(None, "section"),
    )
    return jax.shard_map(
        per_device,
        mesh=mesh,
        in_specs=placed,
        out_specs=P(None, None, None, "lon", "section"),
        check_vma=False,
    )
```

time: 104 us -> 83.8 us (0.81)
  the two profiles are of different devices: /device:TPU:5 before, /device:TPU:4 now
where the time goes in v2:
time: 83.8 us; the launch traced here: 83.6 us
  Pallas kernels  81.8 us (98%)
  local copies, waits for them, and re-layouts  1.77 us (2%)
    pallas_call x1, Pallas kernels, per_device(): pl.pallas_call(functools.partial(kernel, micro), out_shape=jax.ShapeDtype...  81.8 us
    transpose x1, local copies, waits for them, and re-layouts, per_device(): decoded.transpose(0, 5, 1, 3, 2, 4, 6)  1.77 us

profile of v2, /device:TPU:4, one launch (start us, length us, event | category | flops | bytes accessed | tf_op | source)
XLA Modules:
  0.0 83.6 jit_solution(16774651930862298026)
XLA Ops:
  0.0 81.8 %shard_map.55 = bf16[6,2,72,128]{3,2,1,0:T(8,128)(2,1)} custom-call(bf16[3,12,12,2,512]{4,3,2,1,0:T(2,128)(2,1)} %bitcast.6, f32[1,512]{1,0:T(1,128)} %gain_ref.1, bf16[1,512,1536]{2,1,0:T(8,128)(2,1)} %wqkv_ref.1, bf16[1,512,512]{2,1,0:T(8,128)(2,1)} %wout_ref.1, bf16[512,128]{1,0:T(8,128)(2,1)} %whead_ref.1), custom_call_target="tpu_custom_call" | custom-call | tf_op jit(solution)/shard_map/pallas_call | solution.py:415
  81.9 1.8 %copy.6 = bf16[3,2,2,6,2,6,128]{6,1,5,4,3,2,0:T(2,128)(2,1)} copy(bf16[3,2,2,6,2,6,128]{6,1,5,3,4,2,0:T(2,128)(2,1)} %bitcast.5) | data formatting | bytes 442368 | tf_op jit(solution)/shard_map/transpose | solution.py:452

commit v3 on v2

v3 whole, which is shorter than its diff:
```python
import functools

import jax
import jax.numpy as jnp
from jax import lax
from jax.experimental import pallas as pl
from jax.experimental.pallas import tpu as pltpu
from jax.sharding import PartitionSpec as P

MESH = pl.DeviceIdType.MESH
F32, BF16 = jnp.float32, jnp.bfloat16
HEADS = 8
HALF = 72
WIN = 2 * HALF
EPS = 1e-05
LAYERS = 8
SKIP = 5
LANES = 128


def dot(a, b):
    return jnp.dot(a, b, preferred_element_type=F32)


def dot_t(a, b):
    return lax.dot_general(a, b, (((1,), (1,)), ((), ())), preferred_element_type=F32)


def normalize(x, gain):
    mean = jnp.mean(x, axis=-1, keepdims=True)
    centred = x - mean
    spread = jnp.mean(centred * centred, axis=-1, keepdims=True)
    return (centred * lax.rsqrt(spread + EPS) * gain).astype(BF16)


def attend(query, kv, width):
    rows = query.shape[0]
    low = lax.broadcasted_iota(jnp.int32, (rows, LANES), 1) < LANES // 2
    weights = []
    for pair in range(width // LANES):
        cols = slice(pair * LANES, (pair + 1) * LANES)
        q = query[:, cols]
        both = jnp.concatenate([jnp.where(low, q, 0.0), jnp.where(low, 0.0, q)], 0).astype(BF16)
        scores = dot_t(both, kv[:, cols])
        top = jnp.max(scores, axis=-1, keepdims=True)
        weights.append(jnp.exp2(scores - top).astype(BF16))
    mixed = []
    for pair in range(width // LANES):
        values = kv[:, width + pair * LANES : width + (pair + 1) * LANES]
        summed = dot(weights[pair], jnp.concatenate([values, jnp.ones_like(values)], 1))
        summed = summed[:, :LANES] / summed[:, LANES:]
        mixed.append(jnp.where(low, summed[:rows], summed[rows:]))
    return jnp.concatenate(mixed, 1).astype(BF16)


def split(lon, lons):
    low = lax.rem(lon, 2)
    high = lon // (lons // 2)
    return high, lon - low - high * (lons // 2), low


def crossed(high, middle, low, lons):
    flip = jnp.where(middle == lons // 2 - 2, low, 1 - low)
    return high + flip - 2 * high * flip


def holder(layer, block, lons):
    block = lax.rem(block + lons, lons)
    high, middle, low = split(block, lons)
    first = (0, block)
    second = (1, crossed(high, middle, low, lons) * (lons // 2) + middle + low)
    later = (2 * (layer // 2) + low, block - low + lax.rem(layer, 2))
    return tuple(jnp.where(layer == 0, f, jnp.where(layer == 1, g, h)) for f, g, h in zip(first, second, later))


def role(sec, lon, lons):
    high, middle, low = split(lon, lons)
    side = lax.rem(sec, 2)
    layer = jnp.where(sec < 2, sec, sec - side + low)
    beside = crossed(high, middle, low, lons) * (lons // 2) + middle + low
    block = jnp.where(sec == 0, lon, jnp.where(sec == 1, beside, lon - low + side))
    return layer, block


def kernel(micro, x_ref, gain_ref, wqkv_ref, wout_ref, whead_ref, out_ref,
           xin, gain, wqkv, wout, whead, xs, kv, arrived, skips, relayed, sent, outs,
           load_sem, arrive_sem, send_sem, skip_sem, skipsend_sem, head_sem, headsend_sem, out_sem, outsend_sem,
           swap_sem, swapsend_sem, relay_sem, relaysend_sem, share_sem, sharesend_sem):
    sections, lons = lax.axis_size("section"), lax.axis_size("lon")
    sec, lon = lax.axis_index("section"), lax.axis_index("lon")
    layer, mine = role(sec, lon, lons)
    odd = lax.rem(layer, 2)
    width = wout_ref.shape[-1]
    streams = 2 * micro
    last = LAYERS - 1
    core = lax.rem(lon, 2)
    side = lax.rem(sec, 2)
    swaps = jnp.logical_and(sec >= 2, side != core)
    keeps = jnp.logical_not(swaps)

    def target(half, to):
        return holder(to, mine + half - 1 + odd, lons)

    low = lax.rem(mine, 2)
    from_layer, from_block = role(sec - (sections - 2), lon, lons)
    from_odd = lax.rem(from_block, 2)
    relays = jnp.logical_or(sec == sections - 2, jnp.logical_and(sec == sections - 1, from_odd == 1))
    offers = jnp.logical_or(layer == 0, jnp.logical_and(layer == 1, low == 1))
    straight = sec // 2 == 1

    partners = [(sec + 1 - 2 * side, lax.rem(lon + h * (lons // 2), lons) + 1 - 2 * core) for h in range(2)]

    loads = [
        pltpu.make_async_copy(gain_ref, gain, load_sem.at[0]),
        pltpu.make_async_copy(wqkv_ref.at[0], wqkv, load_sem.at[1]),
        pltpu.make_async_copy(wout_ref.at[0], wout, load_sem.at[2]),
    ]

    def load_x(m):
        return pltpu.make_async_copy(x_ref.at[m], xin.at[m], load_sem.at[4 + m])

    pl.when(layer == 0)(lambda: load_x(0).start())

    @pl.when(keeps)
    def _():
        for load in loads:
            load.start()

    load_head = pltpu.make_async_copy(whead_ref, whead.at[side, sec // 2], load_sem.at[3])

    barrier = pltpu.get_barrier_semaphore()

    def greet(where):
        pl.semaphore_signal(barrier, inc=1, device_id=where, device_id_type=MESH)

    def source(behind, half):
        before = layer - behind
        return holder(before, mine - (half - 1 + lax.rem(before + LAYERS, 2)), lons)

    @pl.when(layer > 0)
    def _():
        for half in range(2):
            greet(source(1, half))

    @pl.when(jnp.logical_and(layer == SKIP, low == 0))
    def _():
        greet((sections - 2, mine))
        greet((sections - 2, mine + 1))

    pl.when(jnp.logical_and(layer == SKIP, low == 1))(lambda: greet((sections - 1, holder(jnp.int32(1), mine, lons)[1])))
    pl.when(layer > SKIP)(lambda: greet((sec - 4, lon)))
    pl.when(relays)(lambda: greet((sec - (sections - 2), lon)))

    @pl.when(swaps)
    def _():
        for where in partners:
            greet(where)

    for half in range(2):
        where = holder(jnp.int32(last), lon - half, lons)
        here = jnp.logical_and(where[0] == sec, where[1] == lon)
        pl.when(jnp.logical_not(here))(functools.partial(greet, where))

    @pl.when(layer == last)
    def _():
        for row in range(sections // 2 - 1):
            greet((2 * row + side, lon))
        greet((sec + 1 - 2 * side, lon))

    def place(stream):
        m, lat = stream // 2, lax.rem(stream, 2)
        pl.when(lat == 0)(lambda: load_x(m).wait())
        for half in range(2):
            for a in range(6):
                block = xin[m, lat * 6 + a, half * 6 : half * 6 + 6].astype(F32)
                at = half * HALF + a * 12
                xs[at : at + 12] = block.reshape(12, width)

    count = jnp.where(layer < last, 2, 2 * sections - 1) + jnp.where(swaps, 2, 0)
    for sends in (offers, straight, relays, core == 1):
        count = count + jnp.where(sends, 1, 0)

    @pl.when(layer > 0)
    @jax.named_scope('greet')
    def _():
        pl.semaphore_wait(barrier, count)

    def swap_copy(half, piece):
        where = partners[half]
        rows = pl.ds(half * (width // 2), width // 2)
        src, dst = ((wqkv_ref.at[0, rows], wqkv.at[rows]), (wout_ref.at[0, rows], wout.at[rows]), (gain_ref, gain))[piece]
        return pltpu.make_async_remote_copy(
            src_ref=src, dst_ref=dst, send_sem=swapsend_sem.at[piece], recv_sem=swap_sem.at[piece],
            device_id=where, device_id_type=MESH)

    swap_list = ((0, 2), (0, 0), (1, 0), (0, 1), (1, 1))

    @pl.when(swaps)
    def _():
        for half, piece in swap_list:
            swap_copy(half, piece).start()

    def swap_wait(sems, piece):
        ref = (wqkv, wout, gain)[piece]
        pltpu.make_async_copy(ref, ref, sems.at[piece]).wait()

    def head_copy():
        mine_head = whead.at[side, sec // 2]
        return pltpu.make_async_remote_copy(
            src_ref=mine_head, dst_ref=mine_head, send_sem=headsend_sem, recv_sem=head_sem,
            device_id=(sections - 2 + side, lon), device_id_type=MESH)

    def share_copy():
        return pltpu.make_async_remote_copy(
            src_ref=whead.at[side], dst_ref=whead.at[side], send_sem=sharesend_sem, recv_sem=share_sem,
            device_id=(sec + 1 - 2 * side, lon), device_id_type=MESH)

    sends_head = jnp.logical_and(core == 1, sec < sections - 2)


    @pl.when(keeps)
    def _():
        for load in loads:
            load.wait()

    load_head.start()

    @pl.when(layer == 0)
    def _():
        for m in range(1, micro):
            load_x(m).start()

    def step_copy(stream, half):
        return pltpu.make_async_remote_copy(
            src_ref=sent.at[stream, half], dst_ref=arrived.at[stream, 1 - half],
            send_sem=send_sem, recv_sem=arrive_sem.at[stream, 1 - half],
            device_id=target(half, jnp.minimum(layer + 1, last)), device_id_type=MESH)

    def offer_one(stream):
        return pltpu.make_async_remote_copy(
            src_ref=sent.at[stream, 1 - low], dst_ref=relayed.at[stream, 0],
            send_sem=skipsend_sem, recv_sem=relay_sem.at[stream, 0],
            device_id=(sections - 2, lon), device_id_type=MESH)

    def offer_both(stream, half):
        return pltpu.make_async_remote_copy(
            src_ref=arrived.at[stream, half], dst_ref=relayed.at[stream, half],
            send_sem=skipsend_sem, recv_sem=relay_sem.at[stream, half],
            device_id=(sections - 1, lon), device_id_type=MESH)

    def relay_out(stream, half, slot, block):
        return pltpu.make_async_remote_copy(
            src_ref=relayed.at[stream, half], dst_ref=skips.at[stream, slot],
            send_sem=relaysend_sem, recv_sem=skip_sem.at[stream, slot],
            device_id=holder(jnp.int32(SKIP), block, lons), device_id_type=MESH)

    def skip_copy(stream, half):
        return pltpu.make_async_remote_copy(
            src_ref=arrived.at[stream, half], dst_ref=skips.at[stream, half],
            send_sem=skipsend_sem, recv_sem=skip_sem.at[stream, half],
            device_id=(lax.rem(sec + 4, sections), lon), device_id_type=MESH)

    @jax.named_scope('relay')
    def relay(stream):
        @pl.when(sec == sections - 2)
        def _():
            offer_one(stream).wait_recv()
            relay_out(stream, 0, from_odd, from_block - from_odd).start()

        @pl.when(sec == sections - 1)
        def _():
            for half in range(2):
                offer_both(stream, half).wait_recv()
                relay_out(stream, half, half, from_block).start()

    def out_copy(stream, half, c):
        return pltpu.make_async_remote_copy(
            src_ref=outs.at[(stream * 2 + half) * sections + c], dst_ref=out_ref.at[stream, 1 - half],
            send_sem=outsend_sem, recv_sem=out_sem,
            device_id=(c, lax.rem(mine + half, lons)), device_id_type=MESH)

    def out_local(stream, half, c):
        return pltpu.make_async_copy(outs.at[(stream * 2 + half) * sections + c], out_ref.at[stream, 1 - half], out_sem)

    def stays(half, c):
        return jnp.logical_and(sec == c, lax.rem(mine + half, lons) == lon)

    def out_side(stream, to):
        def send(row, carry):
            c = 2 * row + to
            for half in range(2):
                pl.when(jnp.logical_not(stays(half, c)))(lambda: out_copy(stream, half, c).start())
                pl.when(stays(half, c))(lambda: out_local(stream, half, c).start())
            return carry

        lax.fori_loop(0, sections // 2, send, 0, unroll=True)

    def send_head():
        load_head.wait()
        pl.when(sends_head)(lambda: head_copy().start())

    pl.when(layer > 0)(send_head)

    @pl.when(layer == last)
    @jax.named_scope('share')
    def _():
        others = whead.at[side, pl.ds(0, sections // 2 - 1)]
        pltpu.make_async_copy(others, others, head_sem).wait()
        share_copy().start()

    def relay_all():
        def one(stream, carry):
            relay(stream)
            return carry

        lax.fori_loop(0, streams, one, 0)

    pl.when(relays)(relay_all)

    def step(stream, carry):
        @pl.when(layer > 0)
        @jax.named_scope('arrive')
        def _():
            for half in range(2):
                step_copy(stream, 1 - half).wait_recv()

        pl.when(layer == 0)(lambda: place(stream))

        @pl.when(jnp.logical_and(layer == 1, low == 1))
        def _():
            for half in range(2):
                offer_both(stream, half).start()

        @pl.when(straight)
        def _():
            for half in range(2):
                skip_copy(stream, half).start()

        @pl.when(jnp.logical_and(layer > 0, layer < SKIP))
        def _():
            for half in range(2):
                xs[half * HALF : (half + 1) * HALF] = arrived[stream, half].astype(F32)

        @pl.when(layer >= SKIP)
        def _():
            for half in range(2):
                with jax.named_scope('skip'):
                    skip_copy(stream, half).wait_recv()
                joined = arrived[stream, half].astype(F32) + skips[stream, half].astype(F32)
                xs[half * HALF : (half + 1) * HALF] = joined.astype(BF16).astype(F32)

        def block(before_out):
            x = xs[...]
            normed = normalize(x, gain[...])
            query = dot(normed, wqkv[:, :width]) * ((width // HEADS) ** -0.5 * 1.4426950408889634)
            kv[...] = dot(normed, wqkv[:, width:]).astype(BF16)
            mixed = attend(query, kv, width)
            before_out()
            y = x + dot(mixed, wout[...])
            for half in range(2):
                sent[stream, half] = y[half * HALF : (half + 1) * HALF].astype(BF16)

        first_swapped = jnp.logical_and(swaps, stream == 0)

        @pl.when(first_swapped)
        def _():
            with jax.named_scope('swap'):
                swap_wait(swap_sem, 0)
                swap_wait(swap_sem, 2)
            block(lambda: swap_wait(swap_sem, 1))

        @pl.when(jnp.logical_not(first_swapped))
        @jax.named_scope('block')
        def _():
            block(lambda: None)

        @pl.when(jnp.logical_and(layer == 0, stream == 0))
        @jax.named_scope('greet')
        def _():
            pl.semaphore_wait(barrier, count)

        @pl.when(layer < last)
        def _():
            for half in range(2):
                step_copy(stream, half).start()

        pl.when(layer == 0)(lambda: offer_one(stream).start())
        pl.when(jnp.logical_and(layer == 0, stream == 0))(send_head)

        @pl.when(layer == last)
        @jax.named_scope('head')
        def _():
            @pl.when(stream == 0)
            @jax.named_scope('headwait')
            def _():
                share_copy().wait_recv()

            both = jnp.concatenate([sent[stream, 0].astype(F32), sent[stream, 1].astype(F32)], 0).astype(BF16)
            for pair in range(sections // 2):
                cols = jnp.concatenate([whead[0, pair], whead[1, pair]], 1)
                made = dot(both, cols)
                for part in range(2):
                    piece = made[:, part * LANES : (part + 1) * LANES]
                    for half in range(2):
                        rows = piece[half * HALF : (half + 1) * HALF]
                        outs[(stream * 2 + half) * sections + 2 * pair + part] = rows.astype(BF16)
            pl.when(jnp.logical_and(stream >= 1, stream < streams - 1))(lambda: out_side(stream - 1, 1 - side))
            pl.when(stream >= streams - 2)(lambda: out_side(stream, 1 - side))
            out_side(stream, side)

        return carry

    lax.fori_loop(0, streams, step, 0)

    with jax.named_scope('output'):
        pltpu.make_async_copy(out_ref, out_ref, out_sem).wait()

    @pl.when(layer < last)
    def _():
        pltpu.make_async_copy(sent, sent, send_sem).wait()

    def left(ref, sem):
        pltpu.make_async_copy(ref, ref, sem).wait()

    one_each = pl.ds(0, streams // 2)
    pl.when(layer == 0)(lambda: left(sent.at[one_each], skipsend_sem))
    pl.when(jnp.logical_or(straight, jnp.logical_and(offers, layer == 1)))(lambda: left(arrived, skipsend_sem))
    pl.when(sec == sections - 2)(lambda: left(relayed.at[one_each], relaysend_sem))
    pl.when(jnp.logical_and(relays, sec == sections - 1))(lambda: left(relayed, relaysend_sem))

    @pl.when(layer == last)
    def _():
        most = outs.at[pl.ds(0, streams * (2 * sections - 1))]
        pltpu.make_async_copy(most, most, outsend_sem).wait()

    pl.when(sends_head)(lambda: head_copy().wait_send())

    @pl.when(layer == last)
    def _():
        share_copy().wait_send()

    @pl.when(swaps)
    def _():
        for piece in range(3):
            swap_wait(swapsend_sem, piece)


def per_device(inputs, norm_gain, w_qkv, w_out, w_head):
    inputs = inputs.transpose(0, 2, 3, 1, 4)
    micro, lat, lon, levels, width = inputs.shape
    sections = lax.axis_size("section")
    columns = w_head.shape[1]
    streams = 2 * micro
    dma = pltpu.SemaphoreType.DMA
    hbm = pl.BlockSpec(memory_space=pl.ANY)
    decoded = pl.pallas_call(
        functools.partial(kernel, micro),
        out_shape=jax.ShapeDtypeStruct((streams, 2, HALF, columns), BF16),
        in_specs=[hbm] * 5,
        out_specs=hbm,
        scratch_shapes=[
            pltpu.VMEM(inputs.shape, BF16),
            pltpu.VMEM(norm_gain.shape, F32),
            pltpu.VMEM(w_qkv.shape[1:], BF16),
            pltpu.VMEM(w_out.shape[1:], BF16),
            pltpu.VMEM((2, sections // 2) + w_head.shape, BF16),
            pltpu.VMEM((WIN, width), F32),
            pltpu.VMEM((WIN, 2 * width), BF16),
            pltpu.VMEM((streams, 2, HALF, width), BF16),
            pltpu.VMEM((streams, 2, HALF, width), BF16),
            pltpu.VMEM((streams, 2, HALF, width), BF16),
            pltpu.VMEM((streams, 2, HALF, width), BF16),
            pltpu.VMEM((streams * 2 * sections, HALF, columns), BF16),
            dma((4 + micro,)),
            dma((streams, 2)),
            dma,
            dma((streams, 2)),
            dma,
            dma,
            dma,
            dma,
            dma,
            dma((3,)),
            dma((3,)),
            dma((streams, 2)),
            dma,
            dma,
            dma,
        ],
        compiler_params=pltpu.CompilerParams(
            collective_id=0, has_side_effects=True, vmem_limit_bytes=60 * 2**20
        ),
    )(inputs, norm_gain, w_qkv, w_out, w_head)
    decoded = decoded.reshape(micro, 2, 2, lat // 2, lon // 2, levels, columns)
    return decoded.transpose(0, 5, 1, 3, 2, 4, 6).reshape(micro, levels, lat, lon, columns)


def solution(mesh):
    placed = (
        P(None, None, None, "lon", None),
        P("section", None),
        P("section", None, None),
        P("section", None, None),
        P(None, "section"),
    )
    return jax.shard_map(
        per_device,
        mesh=mesh,
        in_specs=placed,
        out_specs=P(None, None, None, "lon", "section"),
        check_vma=False,
    )
```

time: 83.8 us -> 71.7 us (0.86)
  the two profiles are of different devices: /device:TPU:4 before, /device:TPU:2 now
where the time goes in v3:
time: 71.7 us; the launch traced here: 71.6 us
  Pallas kernels  69.8 us (97%)
  local copies, waits for them, and re-layouts  1.77 us (2%)
    pallas_call x1, Pallas kernels, per_device(): pl.pallas_call(functools.partial(kernel, micro), out_shape=jax.ShapeDtype...  69.8 us
    transpose x1, local copies, waits for them, and re-layouts, per_device(): decoded.transpose(0, 5, 1, 3, 2, 4, 6)  1.77 us

profile of v3, /device:TPU:2, one launch (start us, length us, event | category | flops | bytes accessed | tf_op | source)
XLA Modules:
  0.0 71.6 jit_solution(8501782581593169626)
XLA Ops:
  0.0 69.8 %shard_map.55 = bf16[6,2,72,128]{3,2,1,0:T(8,128)(2,1)} custom-call(bf16[3,12,12,2,512]{4,3,2,1,0:T(2,128)(2,1)} %bitcast.6, f32[1,512]{1,0:T(1,128)} %gain_ref.1, bf16[1,512,1536]{2,1,0:T(8,128)(2,1)} %wqkv_ref.1, bf16[1,512,512]{2,1,0:T(8,128)(2,1)} %wout_ref.1, bf16[512,128]{1,0:T(8,128)(2,1)} %whead_ref.1), custom_call_target="tpu_custom_call" | custom-call | tf_op jit(solution)/shard_map/pallas_call | solution.py:456
  69.8 1.8 %copy.6 = bf16[3,2,2,6,2,6,128]{6,1,5,4,3,2,0:T(2,128)(2,1)} copy(bf16[3,2,2,6,2,6,128]{6,1,5,3,4,2,0:T(2,128)(2,1)} %bitcast.5) | data formatting | bytes 442368 | tf_op jit(solution)/shard_map/transpose | solution.py:495

commit v4 on v3

--- a/solution.py
+++ b/solution.py
@@ -10,6 +10,7 @@
 MESH = pl.DeviceIdType.MESH
 F32, BF16 = jnp.float32, jnp.bfloat16
 HEADS = 8
+PASSED = 4
 HALF = 72
 WIN = 2 * HALF
 EPS = 1e-05
@@ -59,16 +60,23 @@
     return high, lon - low - high * (lons // 2), low
 
 
-def crossed(high, middle, low, lons):
-    flip = jnp.where(middle == lons // 2 - 2, low, 1 - low)
-    return high + flip - 2 * high * flip
+def beside(high, middle, low, lons):
+    flip = 1 - low
+    usual = (high + flip - 2 * high * flip) * (lons // 2) + middle + low
+    return usual, middle == lons // 2 - 2
+
+
+def from_first(block, lons):
+    _, middle, low = split(lax.rem(block + lons, lons), lons)
+    return jnp.logical_or(low == 0, middle == lons // 2 - 2)
 
 
 def holder(layer, block, lons):
     block = lax.rem(block + lons, lons)
     high, middle, low = split(block, lons)
     first = (0, block)
-    second = (1, crossed(high, middle, low, lons) * (lons // 2) + middle + low)
+    usual, at_end = beside(high, middle, low, lons)
+    second = (1, jnp.where(at_end, (1 - low) * (lons // 2) + middle + high, usual))
     later = (2 * (layer // 2) + low, block - low + lax.rem(layer, 2))
     return tuple(jnp.where(layer == 0, f, jnp.where(layer == 1, g, h)) for f, g, h in zip(first, second, later))
 
@@ -77,15 +85,16 @@
     high, middle, low = split(lon, lons)
     side = lax.rem(sec, 2)
     layer = jnp.where(sec < 2, sec, sec - side + low)
-    beside = crossed(high, middle, low, lons) * (lons // 2) + middle + low
-    block = jnp.where(sec == 0, lon, jnp.where(sec == 1, beside, lon - low + side))
+    usual, at_end = beside(high, middle, low, lons)
+    second = jnp.where(at_end, low * (lons // 2) + middle + 1 - high, usual)
+    block = jnp.where(sec == 0, lon, jnp.where(sec == 1, second, lon - low + side))
     return layer, block
 
 
 def kernel(micro, x_ref, gain_ref, wqkv_ref, wout_ref, whead_ref, out_ref,
-           xin, gain, wqkv, wout, whead, xs, kv, arrived, skips, relayed, sent, outs,
+           xin, gain, wqkv, wout, whead, xs, kv, arrived, skips, relayed, sent, outs, passed,
            load_sem, arrive_sem, send_sem, skip_sem, skipsend_sem, head_sem, headsend_sem, out_sem, outsend_sem,
-           swap_sem, swapsend_sem, relay_sem, relaysend_sem, share_sem, sharesend_sem):
+           swap_sem, swapsend_sem, relay_sem, relaysend_sem, share_sem, sharesend_sem, pass_sem, passsend_sem):
     sections, lons = lax.axis_size("section"), lax.axis_size("lon")
     sec, lon = lax.axis_index("section"), lax.axis_index("lon")
     layer, mine = role(sec, lon, lons)
@@ -101,11 +110,17 @@
     def target(half, to):
         return holder(to, mine + half - 1 + odd, lons)
 
-    low = lax.rem(mine, 2)
     from_layer, from_block = role(sec - (sections - 2), lon, lons)
-    from_odd = lax.rem(from_block, 2)
-    relays = jnp.logical_or(sec == sections - 2, jnp.logical_and(sec == sections - 1, from_odd == 1))
-    offers = jnp.logical_or(layer == 0, jnp.logical_and(layer == 1, low == 1))
+
+    def given(block):
+        return [from_first(block + half - 1, lons) for half in range(2)]
+
+    gives = [jnp.logical_and(layer == 0, g) for g in given(mine)]
+    hands = [jnp.logical_and(sec == sections - 2, g) for g in given(from_block)]
+    gives_input = jnp.logical_and(layer == 1, jnp.logical_not(from_first(mine, lons)))
+    hands_input = jnp.logical_and(sec == sections - 1, jnp.logical_not(from_first(from_block, lons)))
+    offers = jnp.logical_or(layer == 0, gives_input)
+    relays = jnp.logical_or(sec == sections - 2, hands_input)
     straight = sec // 2 == 1
 
     partners = [(sec + 1 - 2 * side, lax.rem(lon + h * (lons // 2), lons) + 1 - 2 * core) for h in range(2)]
@@ -123,8 +138,12 @@
 
     @pl.when(keeps)
     def _():
-        for load in loads:
-            load.start()
+        loads[0].start()
+        rows = width // 4
+        for part in range(4):
+            at = pl.ds(part * rows, rows)
+            pltpu.make_async_copy(wqkv_ref.at[0, at], wqkv.at[at], load_sem.at[1]).start()
+        loads[2].start()
 
     load_head = pltpu.make_async_copy(whead_ref, whead.at[side, sec // 2], load_sem.at[3])
 
@@ -142,14 +161,19 @@
         for half in range(2):
             greet(source(1, half))
 
-    @pl.when(jnp.logical_and(layer == SKIP, low == 0))
+    @pl.when(jnp.logical_and(layer == SKIP, from_first(mine, lons)))
     def _():
         greet((sections - 2, mine))
-        greet((sections - 2, mine + 1))
-
-    pl.when(jnp.logical_and(layer == SKIP, low == 1))(lambda: greet((sections - 1, holder(jnp.int32(1), mine, lons)[1])))
+        greet((sections - 2, lax.rem(mine + 1, lons)))
+
+    @pl.when(jnp.logical_and(layer == SKIP, jnp.logical_not(from_first(mine, lons))))
+    def _():
+        greet((sections - 1, holder(jnp.int32(1), mine, lons)[1]))
+
     pl.when(layer > SKIP)(lambda: greet((sec - 4, lon)))
     pl.when(relays)(lambda: greet((sec - (sections - 2), lon)))
+    passes = sec < sections - 2
+    pl.when(passes)(lambda: greet((sec + 1 - 2 * side, lon)))
 
     @pl.when(swaps)
     def _():
@@ -177,7 +201,7 @@
                 xs[at : at + 12] = block.reshape(12, width)
 
     count = jnp.where(layer < last, 2, 2 * sections - 1) + jnp.where(swaps, 2, 0)
-    for sends in (offers, straight, relays, core == 1):
+    for sends in (offers, straight, hands[0], hands[1], hands_input, passes, core == 1):
         count = count + jnp.where(sends, 1, 0)
 
     @pl.when(layer > 0)
@@ -236,17 +260,11 @@
             send_sem=send_sem, recv_sem=arrive_sem.at[stream, 1 - half],
             device_id=target(half, jnp.minimum(layer + 1, last)), device_id_type=MESH)
 
-    def offer_one(stream):
-        return pltpu.make_async_remote_copy(
-            src_ref=sent.at[stream, 1 - low], dst_ref=relayed.at[stream, 0],
-            send_sem=skipsend_sem, recv_sem=relay_sem.at[stream, 0],
-            device_id=(sections - 2, lon), device_id_type=MESH)
-
-    def offer_both(stream, half):
-        return pltpu.make_async_remote_copy(
-            src_ref=arrived.at[stream, half], dst_ref=relayed.at[stream, half],
+    def offer(ref, stream, half):
+        return pltpu.make_async_remote_copy(
+            src_ref=ref.at[stream, half], dst_ref=relayed.at[stream, half],
             send_sem=skipsend_sem, recv_sem=relay_sem.at[stream, half],
-            device_id=(sections - 1, lon), device_id_type=MESH)
+            device_id=(lax.rem(sec + sections - 2, sections), lon), device_id_type=MESH)
 
     def relay_out(stream, half, slot, block):
         return pltpu.make_async_remote_copy(
@@ -262,15 +280,16 @@
 
     @jax.named_scope('relay')
     def relay(stream):
-        @pl.when(sec == sections - 2)
-        def _():
-            offer_one(stream).wait_recv()
-            relay_out(stream, 0, from_odd, from_block - from_odd).start()
-
-        @pl.when(sec == sections - 1)
-        def _():
-            for half in range(2):
-                offer_both(stream, half).wait_recv()
+        for half in range(2):
+            @pl.when(hands[half])
+            def _():
+                offer(sent, stream, half).wait_recv()
+                relay_out(stream, half, 1 - half, from_block + half - 1).start()
+
+        @pl.when(hands_input)
+        def _():
+            for half in range(2):
+                offer(arrived, stream, half).wait_recv()
                 relay_out(stream, half, half, from_block).start()
 
     def out_copy(stream, half, c):
@@ -285,15 +304,25 @@
     def stays(half, c):
         return jnp.logical_and(sec == c, lax.rem(mine + half, lons) == lon)
 
-    def out_side(stream, to):
-        def send(row, carry):
+    def out_side(stream, to, rows=range(sections // 2)):
+        for row in rows:
             c = 2 * row + to
             for half in range(2):
                 pl.when(jnp.logical_not(stays(half, c)))(lambda: out_copy(stream, half, c).start())
                 pl.when(stays(half, c))(lambda: out_local(stream, half, c).start())
-            return carry
-
-        lax.fori_loop(0, sections // 2, send, 0, unroll=True)
+
+    def pass_in(stream, half, row):
+        c = 2 * row + 1 - side
+        return pltpu.make_async_remote_copy(
+            src_ref=outs.at[(stream * 2 + half) * sections + c], dst_ref=passed.at[stream],
+            send_sem=outsend_sem, recv_sem=pass_sem.at[stream],
+            device_id=(2 * row + side, lax.rem(mine + half, lons)), device_id_type=MESH)
+
+    def pass_out(stream):
+        slot = jnp.where(core == side, 1, 0)
+        return pltpu.make_async_remote_copy(
+            src_ref=passed.at[stream], dst_ref=out_ref.at[stream, slot], send_sem=passsend_sem, recv_sem=out_sem,
+            device_id=(sec + 1 - 2 * side, lon), device_id_type=MESH)
 
     def send_head():
         load_head.wait()
@@ -326,15 +355,11 @@
 
         pl.when(layer == 0)(lambda: place(stream))
 
-        @pl.when(jnp.logical_and(layer == 1, low == 1))
-        def _():
-            for half in range(2):
-                offer_both(stream, half).start()
-
-        @pl.when(straight)
-        def _():
-            for half in range(2):
-                skip_copy(stream, half).start()
+        @pl.when(gives_input)
+        def _():
+            for half in range(2):
+                offer(arrived, stream, half).start()
+
 
         @pl.when(jnp.logical_and(layer > 0, layer < SKIP))
         def _():
@@ -384,7 +409,9 @@
             for half in range(2):
                 step_copy(stream, half).start()
 
-        pl.when(layer == 0)(lambda: offer_one(stream).start())
+        for half in range(2):
+            pl.when(gives[half])(offer(sent, stream, half).start)
+
         pl.when(jnp.logical_and(layer == 0, stream == 0))(send_head)
 
         @pl.when(layer == last)
@@ -404,13 +431,38 @@
                     for half in range(2):
                         rows = piece[half * HALF : (half + 1) * HALF]
                         outs[(stream * 2 + half) * sections + 2 * pair + part] = rows.astype(BF16)
-            pl.when(jnp.logical_and(stream >= 1, stream < streams - 1))(lambda: out_side(stream - 1, 1 - side))
-            pl.when(stream >= streams - 2)(lambda: out_side(stream, 1 - side))
+            @pl.when(stream < PASSED)
+            def _():
+                for row in range(sections // 2 - 1):
+                    for half in range(2):
+                        pass_in(stream, half, row).start()
+                out_side(stream, 1 - side, [sections // 2 - 1])
+
+            pl.when(stream >= PASSED)(lambda: out_side(stream, 1 - side))
             out_side(stream, side)
 
         return carry
 
     lax.fori_loop(0, streams, step, 0)
+
+    @pl.when(straight)
+    def _():
+        def send_skips(stream, carry):
+            for half in range(2):
+                skip_copy(stream, half).start()
+            return carry
+
+        lax.fori_loop(0, streams, send_skips, 0)
+
+    @pl.when(passes)
+    @jax.named_scope('pass')
+    def _():
+        def hand(stream, carry):
+            pltpu.make_async_copy(passed.at[stream], passed.at[stream], pass_sem.at[stream]).wait()
+            pass_out(stream).start()
+            return carry
+
+        lax.fori_loop(0, PASSED, hand, 0)
 
     with jax.named_scope('output'):
         pltpu.make_async_copy(out_ref, out_ref, out_sem).wait()
@@ -422,11 +474,16 @@
     def left(ref, sem):
         pltpu.make_async_copy(ref, ref, sem).wait()
 
-    one_each = pl.ds(0, streams // 2)
-    pl.when(layer == 0)(lambda: left(sent.at[one_each], skipsend_sem))
-    pl.when(jnp.logical_or(straight, jnp.logical_and(offers, layer == 1)))(lambda: left(arrived, skipsend_sem))
-    pl.when(sec == sections - 2)(lambda: left(relayed.at[one_each], relaysend_sem))
-    pl.when(jnp.logical_and(relays, sec == sections - 1))(lambda: left(relayed, relaysend_sem))
+    pl.when(passes)(lambda: left(passed, passsend_sem))
+    def left_halves(ref, sem, which):
+        one, both = jnp.logical_xor(*which), jnp.logical_and(*which)
+        pl.when(one)(lambda: left(ref.at[pl.ds(0, streams // 2)], sem))
+        pl.when(both)(lambda: left(ref, sem))
+
+    left_halves(sent, skipsend_sem, gives)
+    left_halves(relayed, relaysend_sem, hands)
+    pl.when(jnp.logical_or(straight, gives_input))(lambda: left(arrived, skipsend_sem))
+    pl.when(hands_input)(lambda: left(relayed, relaysend_sem))
 
     @pl.when(layer == last)
     def _():
@@ -471,6 +528,7 @@
             pltpu.VMEM((streams, 2, HALF, width), BF16),
             pltpu.VMEM((streams, 2, HALF, width), BF16),
             pltpu.VMEM((streams * 2 * sections, HALF, columns), BF16),
+            pltpu.VMEM((PASSED, HALF, columns), BF16),
             dma((4 + micro,)),
             dma((streams, 2)),
             dma,
@@ -485,6 +543,8 @@
             dma((streams, 2)),
             dma,
             dma,
+            dma,
+            dma((PASSED,)),
             dma,
         ],
         compiler_params=pltpu.CompilerParams(

time: 71.7 us -> 70.9 us (0.989)
  Pallas kernels: 69.8 us -> 69 us
    pallas_call x1, Pallas kernels: 69.8 us -> 69 us  [per_device(): pl.pallas_call(functools.partial(kernel, micro), out_shape=jax.ShapeDtype...]
where the time goes in v4:
time: 70.9 us; the launch traced here: 70.8 us
  Pallas kernels  69 us (97%)
  local copies, waits for them, and re-layouts  1.77 us (2%)
    pallas_call x1, Pallas kernels, per_device(): pl.pallas_call(functools.partial(kernel, micro), out_shape=jax.ShapeDtype...  69 us
    transpose x1, local copies, waits for them, and re-layouts, per_device(): decoded.transpose(0, 5, 1, 3, 2, 4, 6)  1.77 us

profile of v4, /device:TPU:2, one launch (start us, length us, event | category | flops | bytes accessed | tf_op | source)
XLA Modules:
  0.0 70.8 jit_solution(5761721801052568537)
XLA Ops:
  0.0 69.0 %shard_map.55 = bf16[6,2,72,128]{3,2,1,0:T(8,128)(2,1)} custom-call(bf16[3,12,12,2,512]{4,3,2,1,0:T(2,128)(2,1)} %bitcast.6, f32[1,512]{1,0:T(1,128)} %gain_ref.1, bf16[1,512,1536]{2,1,0:T(8,128)(2,1)} %wqkv_ref.1, bf16[1,512,512]{2,1,0:T(8,128)(2,1)} %wout_ref.1, bf16[512,128]{1,0:T(8,128)(2,1)} %whead_ref.1), custom_call_target="tpu_custom_call" | custom-call | tf_op jit(solution)/shard_map/pallas_call | solution.py:513
  69.0 1.8 %copy.6 = bf16[3,2,2,6,2,6,128]{6,1,5,4,3,2,0:T(2,128)(2,1)} copy(bf16[3,2,2,6,2,6,128]{6,1,5,3,4,2,0:T(2,128)(2,1)} %bitcast.5) | data formatting | bytes 442368 | tf_op jit(solution)/shard_map/transpose | solution.py:555

commit v5 on v4

--- a/solution.py
+++ b/solution.py
@@ -242,6 +242,8 @@
     sends_head = jnp.logical_and(core == 1, sec < sections - 2)
 
 
+    pl.when(layer == 0)(lambda: place(0))
+
     @pl.when(keeps)
     def _():
         for load in loads:
@@ -308,8 +310,11 @@
         for row in rows:
             c = 2 * row + to
             for half in range(2):
-                pl.when(jnp.logical_not(stays(half, c)))(lambda: out_copy(stream, half, c).start())
-                pl.when(stays(half, c))(lambda: out_local(stream, half, c).start())
+                if row < sections // 2 - 1:
+                    out_copy(stream, half, c).start()
+                else:
+                    pl.when(jnp.logical_not(stays(half, c)))(lambda: out_copy(stream, half, c).start())
+                    pl.when(stays(half, c))(lambda: out_local(stream, half, c).start())
 
     def pass_in(stream, half, row):
         c = 2 * row + 1 - side
@@ -353,7 +358,7 @@
             for half in range(2):
                 step_copy(stream, 1 - half).wait_recv()
 
-        pl.when(layer == 0)(lambda: place(stream))
+        pl.when(jnp.logical_and(layer == 0, stream > 0))(lambda: place(stream))
 
         @pl.when(gives_input)
         def _():
@@ -386,15 +391,20 @@
                 sent[stream, half] = y[half * HALF : (half + 1) * HALF].astype(BF16)
 
         first_swapped = jnp.logical_and(swaps, stream == 0)
+        in_a_hurry = jnp.logical_and(first_swapped, sec < 4)
 
         @pl.when(first_swapped)
-        def _():
-            with jax.named_scope('swap'):
-                swap_wait(swap_sem, 0)
-                swap_wait(swap_sem, 2)
+        @jax.named_scope('swap')
+        def _():
+            swap_wait(swap_sem, 0)
+            swap_wait(swap_sem, 2)
+            pl.when(sec >= 4)(lambda: swap_wait(swap_sem, 1))
+
+        @pl.when(in_a_hurry)
+        def _():
             block(lambda: swap_wait(swap_sem, 1))
 
-        @pl.when(jnp.logical_not(first_swapped))
+        @pl.when(jnp.logical_not(in_a_hurry))
         @jax.named_scope('block')
         def _():
             block(lambda: None)

time: 70.9 us -> 71 us (level)
  no operation moved by 1% of the time
where the time goes in v5:
time: 71 us; the launch traced here: 70.8 us
  Pallas kernels  69 us (97%)
  local copies, waits for them, and re-layouts  1.77 us (2%)
    pallas_call x1, Pallas kernels, per_device(): pl.pallas_call(functools.partial(kernel, micro), out_shape=jax.ShapeDtype...  69 us
    transpose x1, local copies, waits for them, and re-layouts, per_device(): decoded.transpose(0, 5, 1, 3, 2, 4, 6)  1.77 us

profile of v5, /device:TPU:2, one launch (start us, length us, event | category | flops | bytes accessed | tf_op | source)
XLA Modules:
  0.0 70.8 jit_solution(11069890156010506334)
XLA Ops:
  0.0 69.0 %shard_map.55 = bf16[6,2,72,128]{3,2,1,0:T(8,128)(2,1)} custom-call(bf16[3,12,12,2,512]{4,3,2,1,0:T(2,128)(2,1)} %bitcast.6, f32[1,512]{1,0:T(1,128)} %gain_ref.1, bf16[1,512,1536]{2,1,0:T(8,128)(2,1)} %wqkv_ref.1, bf16[1,512,512]{2,1,0:T(8,128)(2,1)} %wout_ref.1, bf16[512,128]{1,0:T(8,128)(2,1)} %whead_ref.1), custom_call_target="tpu_custom_call" | custom-call | tf_op jit(solution)/shard_map/pallas_call | solution.py:523
  69.0 1.8 %copy.6 = bf16[3,2,2,6,2,6,128]{6,1,5,4,3,2,0:T(2,128)(2,1)} copy(bf16[3,2,2,6,2,6,128]{6,1,5,3,4,2,0:T(2,128)(2,1)} %bitcast.5) | data formatting | bytes 442368 | tf_op jit(solution)/shard_map/transpose | solution.py:565

commit v6 on v5

--- a/solution.py
+++ b/solution.py
@@ -10,7 +10,7 @@
 MESH = pl.DeviceIdType.MESH
 F32, BF16 = jnp.float32, jnp.bfloat16
 HEADS = 8
-PASSED = 4
+PASSED = 5
 HALF = 72
 WIN = 2 * HALF
 EPS = 1e-05

time: 71 us -> 71.1 us (level)
  no operation moved by 1% of the time
where the time goes in v6:
time: 71.1 us; the launch traced here: 70.8 us
  Pallas kernels  69 us (97%)
  local copies, waits for them, and re-layouts  1.77 us (2%)
    pallas_call x1, Pallas kernels, per_device(): pl.pallas_call(functools.partial(kernel, micro), out_shape=jax.ShapeDtype...  69 us
    transpose x1, local copies, waits for them, and re-layouts, per_device(): decoded.transpose(0, 5, 1, 3, 2, 4, 6)  1.77 us

profile of v6, /device:TPU:2, one launch (start us, length us, event | category | flops | bytes accessed | tf_op | source)
XLA Modules:
  0.0 70.8 jit_solution(11875645916563442452)
XLA Ops:
  0.0 69.0 %shard_map.55 = bf16[6,2,72,128]{3,2,1,0:T(8,128)(2,1)} custom-call(bf16[3,12,12,2,512]{4,3,2,1,0:T(2,128)(2,1)} %bitcast.6, f32[1,512]{1,0:T(1,128)} %gain_ref.1, bf16[1,512,1536]{2,1,0:T(8,128)(2,1)} %wqkv_ref.1, bf16[1,512,512]{2,1,0:T(8,128)(2,1)} %wout_ref.1, bf16[512,128]{1,0:T(8,128)(2,1)} %whead_ref.1), custom_call_target="tpu_custom_call" | custom-call | tf_op jit(solution)/shard_map/pallas_call | solution.py:523
  69.0 1.8 %copy.6 = bf16[3,2,2,6,2,6,128]{6,1,5,4,3,2,0:T(2,128)(2,1)} copy(bf16[3,2,2,6,2,6,128]{6,1,5,3,4,2,0:T(2,128)(2,1)} %bitcast.5) | data formatting | bytes 442368 | tf_op jit(solution)/shard_map/transpose | solution.py:565
